TPU v7x, 128 devices: a whole 4x4x4 slice. The times are simulated.
128 devices in a mesh: pp: 8 (over x_lo, z), ep: 16 (over y, x_hi, core).
Axes of the slice: x: 4 (x_hi: 2, x_lo: 2; x = x_hi * 2 + x_lo), y: 4, z: 4, core: 2. Of those that a mesh axis runs over, the one named last changes fastest.
Arguments:
- ahead_input: bfloat16 [8, 2048, 7168], P('pp', 'ep'), may hold values from -6 to 6
- ahead_expert: int32 [8, 2048], P('pp', 'ep'), may hold values from 0 to 3, as said below
- ahead_slot: int32 [8, 2048], P('pp', 'ep'), may hold values from 0 to 31, as said below
- ahead_gate: float32 [8, 2048], P('pp', 'ep'), may hold values from 0.25 to 2.5
- back_input: bfloat16 [8, 2048, 7168], P('pp', 'ep'), may hold values from -6 to 6
- back_cotangent: bfloat16 [8, 2048, 7168], P('pp', 'ep'), may hold values from -6 to 6
- back_expert: int32 [8, 2048], P('pp', 'ep'), may hold values from 0 to 3, as said below
- back_slot: int32 [8, 2048], P('pp', 'ep'), may hold values from 0 to 31, as said below
- back_gate: float32 [8, 2048], P('pp', 'ep'), may hold values from 0.25 to 2.5
- gate_weight: bfloat16 [8, 16, 7168, 256], P('pp', 'ep'), may hold values from -0.0625 to 0.0625
- up_weight: bfloat16 [8, 16, 7168, 256], P('pp', 'ep'), may hold values from -0.0625 to 0.0625
- down_weight: bfloat16 [8, 16, 256, 7168], P('pp', 'ep'), may hold values from -0.1875 to 0.1875
Outputs:
- ahead_output: bfloat16 [8, 2048, 7168], P('pp', 'ep')
- back_gradient: bfloat16 [8, 2048, 7168], P('pp', 'ep')
Inputs may be any that keep to these rules, and one draw needn't show every extreme that they name: `ahead_expert`: within the rows of one device (each block of 128 tokens) of each rank, every expert is named by exactly 32 rows. `ahead_slot`: within the rows of one device, the rows that name one expert carry the slots 0 to 31, each once. `back_expert`: within the rows of one device (each block of 128 tokens) of each rank, every expert is named by exactly 32 rows. `back_slot`: within the rows of one device, the rows that name one expert carry the slots 0 to 31, each once.
All inputs are finite; a program needn't handle non-finite values.
Results may differ from a plain program's by a relative error of at most 0.0056.
Values may be sent and summed in bfloat16 or wider, within the bound.
No kernel may reach another device: no remote copies, remote signals or barrier semaphores. Data moves between devices by JAX's collectives and lax.ppermute only.
A program may use at most 192 MiB of HBM per device.

v0:
```python
import functools

import jax
import jax.numpy as jnp
from jax import lax
from jax.experimental import pallas as pl
from jax.experimental.pallas import tpu as pltpu
from jax.sharding import PartitionSpec as P

EPSILON = 1e-06
NY, NX, NC = 4, 2, 2
ORDER = (1, 3, 2, 0)
WIDE = 1024
VMEM = pltpu.CompilerParams(vmem_limit_bytes=40 * 1024 * 1024)
LIGHT = pl.CostEstimate(flops=1000, bytes_accessed=1000, transcendentals=0)


def move(block, dpp=0, dy=0, dx=0, dc=0):
    npp = lax.axis_size("pp")
    nep = lax.axis_size("ep")
    route = []
    for r in range(npp):
        for y in range(NY):
            for x in range(NX):
                for c in range(NC):
                    source = r * nep + (y * NX + x) * NC + c
                    to = ((y + dy) % NY * NX + (x + dx) % NX) * NC + (c + dc) % NC
                    route.append((source, (r + dpp) % npp * nep + to))
    return lax.ppermute(block, ("pp", "ep"), route)


def after(value, *earlier):
    return lax.optimization_barrier((value, *earlier))[0]


def contract_last(left, right):
    return lax.dot_general(
        left, right, (((1,), (1,)), ((), ())), preferred_element_type=jnp.float32
    )


def dot(left, right):
    return jnp.dot(left, right, preferred_element_type=jnp.float32)


def one_hot(positions):
    n = positions.shape[-1]
    index = lax.broadcasted_iota(jnp.int32, (n, n), 0)
    return (index == positions).astype(jnp.bfloat16)


def whole(kernel, outs, *operands, scratch=()):
    return pl.pallas_call(
        kernel,
        out_shape=outs,
        in_specs=[pl.BlockSpec(memory_space=pltpu.VMEM)] * len(operands),
        out_specs=jax.tree.map(lambda _: pl.BlockSpec(memory_space=pltpu.VMEM), outs),
        scratch_shapes=scratch,
        compiler_params=VMEM,
        cost_estimate=LIGHT,
    )(*operands)


def table(rows, features):
    return jax.ShapeDtypeStruct((rows, features), jnp.bfloat16)


def norm_kernel(inputs, expert_order, back_order, normed, kept, scales):
    features = inputs.shape[1]
    to_experts, to_back = one_hot(expert_order[...]), one_hot(back_order[...])
    sums = jnp.zeros((inputs.shape[0], 1), jnp.float32)
    kept_sums = sums
    for j in range(0, features, WIDE):
        values = inputs[:, j : j + WIDE]
        wide = values.astype(jnp.float32)
        sums += jnp.sum(wide * wide, axis=1, keepdims=True)
        moved = dot(to_back, values)
        kept_sums += jnp.sum(moved * moved, axis=1, keepdims=True)
        kept[:, j : j + WIDE] = moved.astype(jnp.bfloat16)
    scale = lax.rsqrt(sums / features + EPSILON)
    scales[...] = lax.rsqrt(kept_sums / features + EPSILON)
    for j in range(0, features, WIDE):
        scaled = (inputs[:, j : j + WIDE].astype(jnp.float32) * scale).astype(jnp.bfloat16)
        normed[:, j : j + WIDE] = dot(to_experts, scaled).astype(jnp.bfloat16)


def norm(inputs, expert_order, back_order):
    rows, features = inputs.shape
    outs = (table(rows, features), table(rows, features), jax.ShapeDtypeStruct((rows, 1), jnp.float32))
    return whole(norm_kernel, outs, inputs, expert_order, back_order)


def pair_kernel(near, far, near_order, far_order, back_order, pairs, kept):
    features = near.shape[1]
    cap = near.shape[0] // NY
    to_near, to_far, to_back = one_hot(near_order[...]), one_hot(far_order[...]), one_hot(back_order[...])
    for j in range(0, features, WIDE):
        here = slice(j, j + WIDE)
        kept[:, here] = dot(to_back, near[:, here]).astype(jnp.bfloat16)
        one = dot(to_near, near[:, here]).astype(jnp.bfloat16)
        two = dot(to_far, far[:, here]).astype(jnp.bfloat16)
        for e in range(NY):
            pairs[2 * e * cap : (2 * e + 1) * cap, here] = one[e * cap : (e + 1) * cap]
            pairs[(2 * e + 1) * cap : (2 * e + 2) * cap, here] = two[e * cap : (e + 1) * cap]


def unpick_kernel(order, *refs):
    *parts, out = refs
    chosen = one_hot(order[...]).T
    for j in range(0, out.shape[1], WIDE):
        rows = jnp.concatenate([p[:, j : j + WIDE] for p in parts], axis=0)
        out[:, j : j + WIDE] = dot(chosen, rows).astype(jnp.bfloat16)


def unpick(order, parts):
    return whole(unpick_kernel, table(order.shape[1], parts[0].shape[1]), order, *parts)


def sum_kernel(near, far, *outs):
    start = 0
    for out in outs:
        here = slice(start, start + out.shape[0])
        for j in range(0, out.shape[1], WIDE):
            across = slice(j, j + WIDE)
            total = near[here, across].astype(jnp.float32) + far[here, across].astype(jnp.float32)
            out[:, across] = total.astype(jnp.bfloat16)
        start += out.shape[0]


def read_total(blocks, summed, across):
    if not summed:
        return jnp.concatenate([b[:, across] for b in blocks], axis=0).astype(jnp.float32)
    return sum(b[:, across].astype(jnp.float32) for b in blocks)


def ahead_kernel(first, summed, kept, gates, *refs):
    *blocks, out = refs
    here = slice(first, first + out.shape[0])
    for j in range(0, out.shape[1], WIDE):
        across = slice(j, j + WIDE)
        total = read_total(blocks, summed, across)
        out[:, across] = (kept[here, across].astype(jnp.float32) + gates[here] * total).astype(jnp.bfloat16)


def back_kernel(first, summed, kept, cotangent, scales, gates, *refs):
    *blocks, out, grads = refs
    rows, features = out.shape
    here = slice(first, first + rows)
    scale = scales[here]
    inner_sum = jnp.zeros((rows, 1), jnp.float32)
    for j in range(0, features, WIDE):
        across = slice(j, j + WIDE)
        grad_normed = gates[here] * read_total(blocks, summed, across)
        grads[:, across] = grad_normed
        inner_sum += jnp.sum(grad_normed * kept[here, across].astype(jnp.float32), axis=1, keepdims=True)
    cubed = scale * scale * scale
    for j in range(0, features, WIDE):
        across = slice(j, j + WIDE)
        values = kept[here, across].astype(jnp.float32)
        grad_layer = (
            scale * grads[:, across]
            - cubed * values * inner_sum / features
            + cotangent[here, across].astype(jnp.float32)
        )
        out[:, across] = grad_layer.astype(jnp.bfloat16)


def by_distance(place, held, turned):
    half = held.shape[0] // 2
    cap = half // NY
    for h in range(2):
        for i, k in enumerate(ORDER):
            start = pl.multiple_of(h * half + (place[0] - k + NY) % NY * cap, cap)
            turned[h * half + i * cap : h * half + (i + 1) * cap] = held[pl.ds(start, cap)]


def store_parts(result, outs):
    start = 0
    for out in outs:
        out[...] = result[start : start + out.shape[0]].astype(jnp.bfloat16)
        start += out.shape[0]


def forward_kernel(steps, place, near, far, g0, g1, u0, u1, d0, d1, *refs):
    *outs, gated, lifted, hidden, turned = refs
    step = pl.program_id(0)
    half = g0.shape[1]

    @pl.when(step == 0)
    def _():
        gated[...] = jnp.zeros_like(gated)
        lifted[...] = jnp.zeros_like(lifted)

    @pl.when(step < steps)
    def _():
        rows = jnp.concatenate([near[...], far[...]], axis=0)
        gated[:, :half] += dot(rows, g0[...])
        gated[:, half:] += dot(rows, g1[...])
        lifted[:, :half] += dot(rows, u0[...])
        lifted[:, half:] += dot(rows, u1[...])

    @pl.when(step == steps - 1)
    def _():
        hidden[...] = (jax.nn.silu(gated[...]) * lifted[...]).astype(jnp.bfloat16)
        by_distance(place, hidden, turned)

    @pl.when(step >= steps)
    def _():
        store_parts(dot(turned[:, :half], d0[...]) + dot(turned[:, half:], d1[...]), outs)


def backward_kernel(steps, place, near, far, pairs, g0, g1, u0, u1, d0, d1, *refs):
    *outs, gated, lifted, upstream, gate_gradient, up_gradient, turned_gate, turned_up = refs
    step = pl.program_id(0)
    half = g0.shape[1]
    tokens = near.shape[0]
    cap = tokens // NY

    @pl.when(step == 0)
    def _():
        gated[...] = jnp.zeros_like(gated)
        lifted[...] = jnp.zeros_like(lifted)
        upstream[...] = jnp.zeros_like(upstream)

    @pl.when(step < steps)
    def _():
        rows = jnp.concatenate([near[...], far[...]], axis=0)
        gated[:, :half] += dot(rows, g0[...])
        gated[:, half:] += dot(rows, g1[...])
        lifted[:, :half] += dot(rows, u0[...])
        lifted[:, half:] += dot(rows, u1[...])
        upstream[:, :half] += contract_last(pairs[...], d0[...])
        upstream[:, half:] += contract_last(pairs[...], d1[...])

    @pl.when(step == steps - 1)
    def _():
        for h in range(2):
            for q in range(NY):
                here = slice(h * tokens + q * cap, h * tokens + (q + 1) * cap)
                gate, lift = gated[here], lifted[here]
                up = upstream[(2 * q + h) * cap : (2 * q + h + 1) * cap]
                sig = jax.nn.sigmoid(gate)
                gate_gradient[here] = (up * lift * sig * (1.0 + gate * (1.0 - sig))).astype(jnp.bfloat16)
                up_gradient[here] = (up * gate * sig).astype(jnp.bfloat16)
        by_distance(place, gate_gradient, turned_gate)
        by_distance(place, up_gradient, turned_up)

    @pl.when(step >= steps)
    def _():
        result = contract_last(turned_gate[:, :half], g0[...]) + contract_last(turned_gate[:, half:], g1[...])
        result += contract_last(turned_up[:, :half], u0[...]) + contract_last(turned_up[:, half:], u1[...])
        store_parts(result, outs)


def through_expert(kernel, place, rows, weights, parts, twice, scratch):
    features = rows[0].shape[1]
    steps = features // WIDE
    first = lambda i: jnp.minimum(i, steps - 1)
    second = lambda i: jnp.maximum(i - steps, 0)
    both = lambda i: i % steps
    gate = [pl.BlockSpec((WIDE, w.shape[1]), lambda i: ((both if twice else first)(i), 0)) for w in weights[:4]]
    down = [pl.BlockSpec((w.shape[0], WIDE), lambda i: (0, (first if twice else second)(i))) for w in weights[4:]]
    return pl.pallas_call(
        functools.partial(kernel, steps),
        grid=(2 * steps,),
        out_shape=[table(n, features) for n in parts],
        in_specs=[pl.BlockSpec(memory_space=pltpu.SMEM)]
        + [pl.BlockSpec((r.shape[0], WIDE), lambda i: (0, first(i))) for r in rows]
        + gate
        + down,
        out_specs=[pl.BlockSpec((n, WIDE), lambda i: (0, second(i))) for n in parts],
        scratch_shapes=scratch,
        compiler_params=VMEM,
        cost_estimate=LIGHT,
    )(place, *rows, *weights)


def body(
    ahead_input,
    ahead_expert,
    ahead_slot,
    ahead_gate,
    back_input,
    back_cotangent,
    back_expert,
    back_slot,
    back_gate,
    gate_weight,
    up_weight,
    down_weight,
):
    tokens, features = ahead_input.shape[1:]
    cap = tokens // NY
    units = gate_weight.shape[3]
    y = lax.axis_index("ep") // (NX * NC)
    place = y.astype(jnp.int32)[None]

    def along_y(rows):
        shape = (NY, rows.shape[0] // NY, features)
        groups = [
            [(q * NX + x) * NC + c for q in range(NY)] for x in range(NX) for c in range(NC)
        ]
        return lax.all_to_all(
            rows.reshape(shape), "ep", 0, 0, axis_index_groups=groups, tiled=True
        ).reshape(rows.shape)

    def cross(rows, *earlier):
        return move(after(rows, *earlier) if earlier else rows, dx=1)

    def positions(expert, slot):
        distance = (expert[0] - y + NY) % NY
        turn = jnp.select([distance == k for k in ORDER], list(range(NY)))
        return (expert * cap + slot), (turn * cap + slot[0])[None]

    ahead_order, ahead_turn = positions(ahead_expert, ahead_slot)
    back_order, back_turn = positions(back_expert, back_slot)
    half = tokens // 2

    far_cotangent = cross(back_cotangent[0])
    far_order = move(back_order, dx=1)
    gate_far = move(gate_weight[0, 0], dc=1)
    up_far = move(up_weight[0, 0], dc=1)
    down_far = move(down_weight[0, 0], dc=1)
    weights = (gate_weight[0, 0], gate_far, up_weight[0, 0], up_far, down_weight[0, 0], down_far)
    ahead_places, back_places = move(ahead_turn, dpp=1), move(back_turn, dpp=-1)

    normed_ahead, ahead_kept, _ = norm(ahead_input[0], ahead_order, ahead_turn)
    ahead_near = along_y(normed_ahead)
    normed_back, back_kept, scales_back = norm(back_input[0], back_order, back_turn)
    back_near = along_y(after(normed_back, ahead_near, far_cotangent, far_order, ahead_places, back_places))

    ahead_far = cross(ahead_near)
    pairs, cotangent_kept = whole(
        pair_kernel,
        (table(2 * tokens, features), table(tokens, features)),
        after(back_cotangent[0], back_near),
        far_cotangent,
        back_order,
        far_order,
        back_turn,
    )
    back_far = cross(back_near, pairs, ahead_far)
    pairs = along_y(pairs)

    groups = (2 * cap, cap, cap)
    wide = lambda dtype: pltpu.VMEM((2 * tokens, 2 * units), dtype)
    partials = through_expert(
        forward_kernel,
        place,
        (ahead_near, ahead_far),
        weights,
        (*groups, *groups),
        False,
        [wide(jnp.float32)] * 2 + [wide(jnp.bfloat16)] * 2,
    )
    ahead_home, ahead_away = partials[:3], partials[3:]
    partials = through_expert(
        backward_kernel,
        after(place, *ahead_home),
        (back_near, back_far, pairs),
        weights,
        (*groups, *groups),
        True,
        [wide(jnp.float32)] * 3 + [wide(jnp.bfloat16)] * 4,
    )
    back_home, back_away = partials[:3], partials[3:]

    def to_owner(home, other, *first):
        blocks = whole(sum_kernel, [table(cap, features)] * (home.shape[0] // cap), home, other)
        return [move(b, dy=-k) for b, k in zip(blocks, first)]

    def in_turn(turn, values):
        chosen = lax.broadcasted_iota(jnp.int32, (tokens, tokens), 0) == turn
        return jnp.sum(jnp.where(chosen, values, 0.0), axis=1, keepdims=True)

    ahead_gates = in_turn(ahead_turn, ahead_gate)
    back_gates = in_turn(back_turn, back_gate)

    def finish_ahead(first, blocks, summed=False):
        rows = cap if summed else cap * len(blocks)
        kernel = functools.partial(ahead_kernel, first * cap, summed)
        return move(whole(kernel, table(rows, features), ahead_kept, ahead_gates, *blocks), dpp=1)

    def finish_back(first, blocks, summed=False):
        rows = cap if summed else cap * len(blocks)
        return move(
            whole(
                functools.partial(back_kernel, first * cap, summed),
                table(rows, features),
                back_kept,
                cotangent_kept,
                scales_back,
                back_gates,
                *blocks,
                scratch=[pltpu.VMEM((rows, features), jnp.float32)],
            ),
            dpp=-1,
        )

    ahead_0 = cross(ahead_away[0], pairs)
    back_0 = cross(back_away[0])
    ahead_sums = to_owner(after(ahead_home[0], back_home[0]), ahead_0, *ORDER[:2])
    back_1 = cross(back_away[1], ahead_0)
    back_sums = to_owner(back_home[0], back_0, *ORDER[:2])
    ahead_1 = cross(ahead_away[1], back_0, *ahead_sums)
    ahead_low = finish_ahead(0, ahead_sums)
    ahead_2 = cross(ahead_away[2], back_1)
    back_sum = to_owner(back_home[1], back_1, *ORDER[2:3])
    back_low = finish_back(0, back_sums)
    back_2 = cross(back_away[2], ahead_1, *back_sums)
    ahead_sum = to_owner(after(ahead_home[1], *back_sum), ahead_1, *ORDER[2:3])
    back_middle = finish_back(2, [after(back_sum[0], ahead_low)])
    ahead_middle = finish_ahead(2, [after(ahead_sum[0], ahead_low)])
    ahead_last = finish_ahead(3, [ahead_home[2], ahead_2], True)
    back_last = finish_back(3, [after(back_home[2], back_low), back_2], True)
    ahead_output = unpick(ahead_places, [ahead_low, ahead_middle, ahead_last])
    back_gradient = unpick(back_places, [back_low, back_middle, back_last])
    return (ahead_output[None], back_gradient[None])


def solution(mesh):
    placed = (
        P("pp", "ep", None),
        P("pp", "ep"),
        P("pp", "ep"),
        P("pp", "ep"),
        P("pp", "ep", None),
        P("pp", "ep", None),
        P("pp", "ep"),
        P("pp", "ep"),
        P("pp", "ep"),
        P("pp", "ep", None, None),
        P("pp", "ep", None, None),
        P("pp", "ep", None, None),
    )
    return jax.shard_map(
        body,
        mesh=mesh,
        in_specs=placed,
        out_specs=(P("pp", "ep", None), P("pp", "ep", None)),
        check_vma=False,
    )
```

profile of v0, /device:TPU:0, one launch (start us, length us, event | category | flops | bytes accessed | tf_op | source)
XLA Modules:
  0.0 271.1 jit_solution(897089491734722426)
XLA Ops:
  0.6 3.2 %collective-permute-start.5 = (bf16[128,7168]{1,0:T(8,128)(2,1)}, bf16[128,7168]{1,0:T(8,128)(2,1)}, u32[]{:S(2)}, u32[]{:S(2)}) collective-permute-start(bf16[128,7168]{1,0:T(8,128)(2,1)} %bitcast.29), channel_id=1, source_target_pairs={{0,2},{1,3},{2,0},{3,1},{4,6},{5,7},{6,4},{7,5},{8,10},{9,11},{10,... | collective-permute-start | bytes 5505032 | tf_op jit(solution)/shard_map/ppermute | solution.py:29
  10.9 4.6 %all-to-all-start = ((bf16[4,32,7168]{2,1,0:T(8,128)(2,1)}), bf16[4,32,7168]{2,1,0:T(8,128)(2,1)}, u32[]{:S(2)}, u32[]{:S(2)}) async-start(bf16[4,32,7168]{2,1,0:T(8,128)(2,1)} %bitcast.31), calls=%async_computation | async-start | bytes 3670016 | tf_op jit(solution)/shard_map/all_to_all | solution.py:303
  27.8 15.7 %collective-permute-done.7.order = s32[1,128]{1,0:T(1,128)S(1)} collective-permute-done((s32[1,128]{1,0:T(1,128)S(1)}, s32[1,128]{1,0:T(1,128)S(1)}, u32[]{:S(2)}, u32[]{:S(2)}) %collective-permute-start.7) | collective-permute-done | bytes 544 | tf_op jit(solution)/shard_map/ppermute | solution.py:29
  43.4 4.4 %collective-permute-done.order = s32[1,128]{1,0:T(1,128)S(1)} collective-permute-done((s32[1,128]{1,0:T(1,128)S(1)}, s32[1,128]{1,0:T(1,128)S(1)}, u32[]{:S(2)}, u32[]{:S(2)}) %collective-permute-start) | collective-permute-done | bytes 544 | tf_op jit(solution)/shard_map/ppermute | solution.py:29
  47.8 4.5 %all-to-all-start.1 = ((bf16[4,32,7168]{2,1,0:T(8,128)(2,1)}), bf16[4,32,7168]{2,1,0:T(8,128)(2,1)}, u32[]{:S(2)}, u32[]{:S(2)}) async-start(bf16[4,32,7168]{2,1,0:T(8,128)(2,1)} %bitcast.32), calls=%async_computation.1 | async-start | bytes 3670016 | tf_op jit(solution)/shard_map/all_to_all | solution.py:303
  54.9 20.0 %all-to-all-done.1 = bf16[4,32,7168]{2,1,0:T(8,128)(2,1)} async-done(((bf16[4,32,7168]{2,1,0:T(8,128)(2,1)}), bf16[4,32,7168]{2,1,0:T(8,128)(2,1)}, u32[]{:S(2)}, u32[]{:S(2)}) %all-to-all-start.1) | async-done | bytes 1835040 | tf_op jit(solution)/shard_map/all_to_all | solution.py:303
  76.4 3.1 %shard_map.134 = (bf16[256,7168]{1,0:T(8,128)(2,1)S(1)}, bf16[128,7168]{1,0:T(8,128)(2,1)S(1)}) custom-call(bf16[128,7168]{1,0:T(8,128)(2,1)S(1)} %bitcast.30, bf16[128,7168]{1,0:T(8,128)(2,1)} %collective-permute-done.5.far, s32[1,128]{1,0:T(1,128)S(1)} %multiply_add_fusion.expert_order.near_order, s32[1,128]{1,0:T(1,128)S(1)} %collective-permute-done.6.far_order, ...), custom_call_target="tpu_custom_call" | custom-call | flops 1000 | bytes 1000 | tf_op jit(solution)/shard_map/pallas_call | solution.py:53
  82.6 4.8 %all-to-all-start.2 = ((bf16[4,64,7168]{2,1,0:T(8,128)(2,1)}), bf16[4,64,7168]{2,1,0:T(8,128)(2,1)}, u32[]{:S(2)}, u32[]{:S(2)}) async-start(bf16[4,64,7168]{2,1,0:T(8,128)(2,1)} %bitcast.28), calls=%async_computation.2 | async-start | bytes 7340032 | tf_op jit(solution)/shard_map/all_to_all | solution.py:303
  87.3 9.8 %collective-permute-done.1.far = bf16[128,7168]{1,0:T(8,128)(2,1)} collective-permute-done((bf16[128,7168]{1,0:T(8,128)(2,1)}, bf16[128,7168]{1,0:T(8,128)(2,1)}, u32[]{:S(2)}, u32[]{:S(2)}) %collective-permute-start.1) | collective-permute-done | bytes 1835040 | tf_op jit(solution)/shard_map/ppermute | solution.py:29
  101.1 15.8 %shard_map.132 = (bf16[64,7168]{1,0:T(8,128)(2,1)S(1)}, bf16[32,7168]{1,0:T(8,128)(2,1)S(1)}, bf16[32,7168]{1,0:T(8,128)(2,1)S(1)}, bf16[64,7168]{1,0:T(8,128)(2...) custom-call(s32[1]{0:T(128)} %bitcast.5.place, bf16[128,7168]{1,0:T(8,128)(2,1)} %bitcast.7.near, ...), custom_call_target="tpu_custom_call" | custom-call | flops 1000 | bytes 1000 | tf_op jit(solution)/shard_map/pallas_call | solution.py:263
  121.0 7.6 %all-to-all-done.2 = bf16[4,64,7168]{2,1,0:T(8,128)(2,1)} async-done(((bf16[4,64,7168]{2,1,0:T(8,128)(2,1)}), bf16[4,64,7168]{2,1,0:T(8,128)(2,1)}, u32[]{:S(2)}, u32[]{:S(2)}) %all-to-all-start.2) | async-done | bytes 3670048 | tf_op jit(solution)/shard_map/all_to_all | solution.py:303
  130.6 11.2 %collective-permute-done.8.far = bf16[128,7168]{1,0:T(8,128)(2,1)} collective-permute-done((bf16[128,7168]{1,0:T(8,128)(2,1)}, bf16[128,7168]{1,0:T(8,128)(2,1)}, u32[]{:S(2)}, u32[]{:S(2)}) %collective-permute-start.8) | collective-permute-done | bytes 1835040 | tf_op jit(solution)/shard_map/ppermute | solution.py:29
  141.8 22.2 %shard_map.135 = (bf16[64,7168]{1,0:T(8,128)(2,1)S(1)}, bf16[32,7168]{1,0:T(8,128)(2,1)S(1)}, bf16[32,7168]{1,0:T(8,128)(2,1)S(1)}, bf16[64,7168]{1,0:T(8,128)(2...) custom-call(s32[1]{0:T(128)} %bitcast.5.place, bf16[128,7168]{1,0:T(8,128)(2,1)} %bitcast.16.near, ...), custom_call_target="tpu_custom_call" | custom-call | flops 1000 | bytes 1000 | tf_op jit(solution)/shard_map/pallas_call | solution.py:263
  167.3 3.2 %collective-permute-start.10 = (bf16[32,7168]{1,0:T(8,128)(2,1)}, bf16[32,7168]{1,0:T(8,128)(2,1)S(1)}, u32[]{:S(2)}, u32[]{:S(2)}) collective-permute-start(bf16[32,7168]{1,0:T(8,128)(2,1)} %get-tuple-element.58), channel_id=1, source_target_pairs={{0,12},{1,13},{2,14},{3,15},{4,0},{5,1},{6,2},{7,3},{8,4},{9,5},{1... | collective-permute-start | bytes 1376264 | tf_op jit(solution)/shard_map/ppermute | solution.py:29
  170.5 14.8 %collective-permute-done.15.far = bf16[64,7168]{1,0:T(8,128)(2,1)S(1)} collective-permute-done((bf16[64,7168]{1,0:T(8,128)(2,1)S(1)}, bf16[64,7168]{1,0:T(8,128)(2,1)S(1)}, u32[]{:S(2)}, u32[]{:S(2)}) %collective-permute-start.15) | collective-permute-done | bytes 917536 | tf_op jit(solution)/shard_map/ppermute | solution.py:29
  186.3 3.4 %collective-permute-start.21 = (bf16[32,7168]{1,0:T(8,128)(2,1)}, bf16[32,7168]{1,0:T(8,128)(2,1)}, u32[]{:S(2)}, u32[]{:S(2)}) collective-permute-start(bf16[32,7168]{1,0:T(8,128)(2,1)} %get-tuple-element.73), channel_id=1, source_target_pairs={{0,12},{1,13},{2,14},{3,15},{4,0},{5,1},{6,2},{7,3},{8,4},{9,5},{1... | collective-permute-start | bytes 1376264 | tf_op jit(solution)/shard_map/ppermute | solution.py:29
  196.6 3.4 %collective-permute-done.22.refs_1_ = bf16[32,7168]{1,0:T(8,128)(2,1)} collective-permute-done((bf16[32,7168]{1,0:T(8,128)(2,1)}, bf16[32,7168]{1,0:T(8,128)(2,1)}, u32[]{:S(2)}, u32[]{:S(2)}) %collective-permute-start.22) | collective-permute-done | bytes 458784 | tf_op jit(solution)/shard_map/ppermute | solution.py:29
  210.6 4.2 %collective-permute-done.16.far = bf16[32,7168]{1,0:T(8,128)(2,1)S(1)} collective-permute-done((bf16[32,7168]{1,0:T(8,128)(2,1)}, bf16[32,7168]{1,0:T(8,128)(2,1)S(1)}, u32[]{:S(2)}, u32[]{:S(2)}) %collective-permute-start.16) | collective-permute-done | bytes 458784 | tf_op jit(solution)/shard_map/ppermute | solution.py:29
  218.5 4.1 %collective-permute-start.17 = (bf16[32,7168]{1,0:T(8,128)(2,1)S(1)}, bf16[32,7168]{1,0:T(8,128)(2,1)S(1)}, u32[]{:S(2)}, u32[]{:S(2)}) collective-permute-start(bf16[32,7168]{1,0:T(8,128)(2,1)S(1)} %shard_map.139), channel_id=1, source_target_pairs={{0,8},{1,9},{2,10},{3,11},{4,12},{5,13},{6,14},{7,15},{8,0},{9,1},... | collective-permute-start | bytes 1376264 | tf_op jit(solution)/shard_map/ppermute | solution.py:29
  222.6 21.6 %collective-permute-done.19.refs_1_ = bf16[32,7168]{1,0:T(8,128)(2,1)S(1)} collective-permute-done((bf16[32,7168]{1,0:T(8,128)(2,1)S(1)}, bf16[32,7168]{1,0:T(8,128)(2,1)S(1)}, u32[]{:S(2)}, u32[]{:S(2)}) %collective-permute-start.19) | collective-permute-done | bytes 458784 | tf_op jit(solution)/shard_map/ppermute | solution.py:29
  245.4 4.2 %collective-permute-start.24 = (bf16[32,7168]{1,0:T(8,128)(2,1)S(1)}, bf16[32,7168]{1,0:T(8,128)(2,1)S(1)}, u32[]{:S(2)}, u32[]{:S(2)}) collective-permute-start(bf16[32,7168]{1,0:T(8,128)(2,1)S(1)} %shard_map.145), channel_id=1, source_target_pairs={{0,112},{1,113},{2,114},{3,115},{4,116},{5,117},{6,118},{7,119},{8... | collective-permute-start | bytes 1376264 | tf_op jit(solution)/shard_map/ppermute | solution.py:29
  249.6 4.5 %collective-permute-done.25.refs_1_ = bf16[32,7168]{1,0:T(8,128)(2,1)S(1)} collective-permute-done((bf16[32,7168]{1,0:T(8,128)(2,1)S(1)}, bf16[32,7168]{1,0:T(8,128)(2,1)S(1)}, u32[]{:S(2)}, u32[]{:S(2)}) %collective-permute-start.25) | collective-permute-done | bytes 458784 | tf_op jit(solution)/shard_map/ppermute | solution.py:29
  257.2 4.7 %collective-permute-done.24.refs_1_ = bf16[32,7168]{1,0:T(8,128)(2,1)S(1)} collective-permute-done((bf16[32,7168]{1,0:T(8,128)(2,1)S(1)}, bf16[32,7168]{1,0:T(8,128)(2,1)S(1)}, u32[]{:S(2)}, u32[]{:S(2)}) %collective-permute-start.24) | collective-permute-done | bytes 458784 | tf_op jit(solution)/shard_map/ppermute | solution.py:29
  261.9 5.2 %collective-permute-done.26.refs_2_ = bf16[32,7168]{1,0:T(8,128)(2,1)S(1)} collective-permute-done((bf16[32,7168]{1,0:T(8,128)(2,1)S(1)}, bf16[32,7168]{1,0:T(8,128)(2,1)S(1)}, u32[]{:S(2)}, u32[]{:S(2)}) %collective-permute-start.26) | collective-permute-done | bytes 458784 | tf_op jit(solution)/shard_map/ppermute | solution.py:29
  (124 shorter events, 70.2 us)
Async XLA Ops:
  0.6 47.2 %collective-permute-start.5 = (bf16[128,7168]{1,0:T(8,128)(2,1)}, bf16[128,7168]{1,0:T(8,128)(2,1)}, u32[]{:S(2)}, u32[]{:S(2)}) collective-permute-start(bf16[128,7168]{1,0:T(8,128)(2,1)} %bitcast.29), channel_id=1, source_target_pairs={{0,2},{1,3},{2,0},{3,1},{4,6},{5,7},{6,4},{7,5},{8,10},{9,11},{10,... | collective-permute-start | bytes 5505032 | tf_op jit(solution)/shard_map/ppermute | solution.py:29
  10.9 37.0 %all-to-all-start = ((bf16[4,32,7168]{2,1,0:T(8,128)(2,1)}), bf16[4,32,7168]{2,1,0:T(8,128)(2,1)}, u32[]{:S(2)}, u32[]{:S(2)}) async-start(bf16[4,32,7168]{2,1,0:T(8,128)(2,1)} %bitcast.31), calls=%async_computation | async-start | bytes 3670016 | tf_op jit(solution)/shard_map/all_to_all | solution.py:303
  15.5 32.4 %collective-permute-start = (s32[1,128]{1,0:T(1,128)S(1)}, s32[1,128]{1,0:T(1,128)S(1)}, u32[]{:S(2)}, u32[]{:S(2)}) collective-permute-start(s32[1,128]{1,0:T(1,128)S(1)} %bitcast.39), channel_id=1, source_target_pairs={{0,16},{1,17},{2,18},{3,19},{4,20},{5,21},{6,22},{7,23},{8,24},{9,... | collective-permute-start | bytes 1544 | tf_op jit(solution)/shard_map/ppermute | solution.py:29
  18.0 25.4 %collective-permute-start.7 = (s32[1,128]{1,0:T(1,128)S(1)}, s32[1,128]{1,0:T(1,128)S(1)}, u32[]{:S(2)}, u32[]{:S(2)}) collective-permute-start(s32[1,128]{1,0:T(1,128)S(1)} %bitcast.35), channel_id=1, source_target_pairs={{0,112},{1,113},{2,114},{3,115},{4,116},{5,117},{6,118},{7,119},{8... | collective-permute-start | bytes 1544 | tf_op jit(solution)/shard_map/ppermute | solution.py:29
  20.3 27.5 %collective-permute-start.6 = (s32[1,128]{1,0:T(1,128)S(1)}, s32[1,128]{1,0:T(1,128)S(1)}, u32[]{:S(2)}, u32[]{:S(2)}) collective-permute-start(s32[1,128]{1,0:T(1,128)S(1)} %multiply_add_fusion.expert_order.near_order), channel_id=1, source_target_pairs={{0,2},{1,3},{2,0},{3,1},{4,6},{5,7},{6,4},{7,5},{8,10},{9,11},{10,... | collective-permute-start | bytes 1544 | tf_op jit(solution)/shard_map/ppermute | solution.py:29
  47.8 27.1 %all-to-all-start.1 = ((bf16[4,32,7168]{2,1,0:T(8,128)(2,1)}), bf16[4,32,7168]{2,1,0:T(8,128)(2,1)}, u32[]{:S(2)}, u32[]{:S(2)}) async-start(bf16[4,32,7168]{2,1,0:T(8,128)(2,1)} %bitcast.32), calls=%async_computation.1 | async-start | bytes 3670016 | tf_op jit(solution)/shard_map/all_to_all | solution.py:303
  52.3 46.8 %collective-permute-start.2 = (bf16[7168,256]{1,0:T(8,128)(2,1)}, bf16[7168,256]{1,0:T(8,128)(2,1)}, u32[]{:S(2)}, u32[]{:S(2)}) collective-permute-start(bf16[7168,256]{1,0:T(8,128)(2,1)} %bitcast.25), channel_id=1, source_target_pairs={{0,1},{1,0},{2,3},{3,2},{4,5},{5,4},{6,7},{7,6},{8,9},{9,8},{10,11... | collective-permute-start | bytes 11010056 | tf_op jit(solution)/shard_map/ppermute | solution.py:29
  52.3 46.8 %collective-permute-start.3 = (bf16[7168,256]{1,0:T(8,128)(2,1)}, bf16[7168,256]{1,0:T(8,128)(2,1)}, u32[]{:S(2)}, u32[]{:S(2)}) collective-permute-start(bf16[7168,256]{1,0:T(8,128)(2,1)} %bitcast.40), channel_id=1, source_target_pairs={{0,1},{1,0},{2,3},{3,2},{4,5},{5,4},{6,7},{7,6},{8,9},{9,8},{10,11... | collective-permute-start | bytes 11010056 | tf_op jit(solution)/shard_map/ppermute | solution.py:29
  52.8 46.3 %collective-permute-start.4 = (bf16[256,7168]{1,0:T(8,128)(2,1)}, bf16[256,7168]{1,0:T(8,128)(2,1)}, u32[]{:S(2)}, u32[]{:S(2)}) collective-permute-start(bf16[256,7168]{1,0:T(8,128)(2,1)} %bitcast.43), channel_id=1, source_target_pairs={{0,1},{1,0},{2,3},{3,2},{4,5},{5,4},{6,7},{7,6},{8,9},{9,8},{10,11... | collective-permute-start | bytes 11010056 | tf_op jit(solution)/shard_map/ppermute | solution.py:29
  52.9 44.2 %collective-permute-start.1 = (bf16[128,7168]{1,0:T(8,128)(2,1)}, bf16[128,7168]{1,0:T(8,128)(2,1)}, u32[]{:S(2)}, u32[]{:S(2)}) collective-permute-start(bf16[128,7168]{1,0:T(8,128)(2,1)} %bitcast.7.near), channel_id=1, source_target_pairs={{0,2},{1,3},{2,0},{3,1},{4,6},{5,7},{6,4},{7,5},{8,10},{9,11},{10,... | collective-permute-start | bytes 5505032 | tf_op jit(solution)/shard_map/ppermute | solution.py:29
  82.6 46.1 %all-to-all-start.2 = ((bf16[4,64,7168]{2,1,0:T(8,128)(2,1)}), bf16[4,64,7168]{2,1,0:T(8,128)(2,1)}, u32[]{:S(2)}, u32[]{:S(2)}) async-start(bf16[4,64,7168]{2,1,0:T(8,128)(2,1)} %bitcast.28), calls=%async_computation.2 | async-start | bytes 7340032 | tf_op jit(solution)/shard_map/all_to_all | solution.py:303
  97.1 44.7 %collective-permute-start.8 = (bf16[128,7168]{1,0:T(8,128)(2,1)}, bf16[128,7168]{1,0:T(8,128)(2,1)}, u32[]{:S(2)}, u32[]{:S(2)}) collective-permute-start(bf16[128,7168]{1,0:T(8,128)(2,1)} %bitcast.16.near), channel_id=1, source_target_pairs={{0,2},{1,3},{2,0},{3,1},{4,6},{5,7},{6,4},{7,5},{8,10},{9,11},{10,... | collective-permute-start | bytes 5505032 | tf_op jit(solution)/shard_map/ppermute | solution.py:29
  128.6 37.5 %collective-permute-start.9 = (bf16[64,7168]{1,0:T(8,128)(2,1)}, bf16[64,7168]{1,0:T(8,128)(2,1)S(1)}, u32[]{:S(2)}, u32[]{:S(2)}) collective-permute-start(bf16[64,7168]{1,0:T(8,128)(2,1)} %copy-done.17), channel_id=1, source_target_pairs={{0,2},{1,3},{2,0},{3,1},{4,6},{5,7},{6,4},{7,5},{8,10},{9,11},{10,... | collective-permute-start | bytes 2752520 | tf_op jit(solution)/shard_map/ppermute | solution.py:29
  164.1 21.2 %collective-permute-start.15 = (bf16[64,7168]{1,0:T(8,128)(2,1)S(1)}, bf16[64,7168]{1,0:T(8,128)(2,1)S(1)}, u32[]{:S(2)}, u32[]{:S(2)}) collective-permute-start(bf16[64,7168]{1,0:T(8,128)(2,1)S(1)} %get-tuple-element.65), channel_id=1, source_target_pairs={{0,2},{1,3},{2,0},{3,1},{4,6},{5,7},{6,4},{7,5},{8,10},{9,11},{10,... | collective-permute-start | bytes 2752520 | tf_op jit(solution)/shard_map/ppermute | solution.py:29
  167.3 25.0 %collective-permute-start.10 = (bf16[32,7168]{1,0:T(8,128)(2,1)}, bf16[32,7168]{1,0:T(8,128)(2,1)S(1)}, u32[]{:S(2)}, u32[]{:S(2)}) collective-permute-start(bf16[32,7168]{1,0:T(8,128)(2,1)} %get-tuple-element.58), channel_id=1, source_target_pairs={{0,12},{1,13},{2,14},{3,15},{4,0},{5,1},{6,2},{7,3},{8,4},{9,5},{1... | collective-permute-start | bytes 1376264 | tf_op jit(solution)/shard_map/ppermute | solution.py:29
  170.5 21.8 %collective-permute-start.11 = (bf16[32,7168]{1,0:T(8,128)(2,1)}, bf16[32,7168]{1,0:T(8,128)(2,1)}, u32[]{:S(2)}, u32[]{:S(2)}) collective-permute-start(bf16[32,7168]{1,0:T(8,128)(2,1)} %get-tuple-element.59), channel_id=1, source_target_pairs={{0,4},{1,5},{2,6},{3,7},{4,8},{5,9},{6,10},{7,11},{8,12},{9,13},{1... | collective-permute-start | bytes 1376264 | tf_op jit(solution)/shard_map/ppermute | solution.py:29
  192.2 22.5 %collective-permute-start.16 = (bf16[32,7168]{1,0:T(8,128)(2,1)}, bf16[32,7168]{1,0:T(8,128)(2,1)S(1)}, u32[]{:S(2)}, u32[]{:S(2)}) collective-permute-start(bf16[32,7168]{1,0:T(8,128)(2,1)} %copy-done.22), channel_id=1, source_target_pairs={{0,2},{1,3},{2,0},{3,1},{4,6},{5,7},{6,4},{7,5},{8,10},{9,11},{10,... | collective-permute-start | bytes 1376264 | tf_op jit(solution)/shard_map/ppermute | solution.py:29
  195.4 49.2 %collective-permute-start.12 = (bf16[64,7168]{1,0:T(8,128)(2,1)S(1)}, bf16[64,7168]{1,0:T(8,128)(2,1)S(1)}, u32[]{:S(2)}, u32[]{:S(2)}) collective-permute-start(bf16[64,7168]{1,0:T(8,128)(2,1)S(1)} %shard_map.137), channel_id=1, source_target_pairs={{0,16},{1,17},{2,18},{3,19},{4,20},{5,21},{6,22},{7,23},{8,24},{9,... | collective-permute-start | bytes 2752520 | tf_op jit(solution)/shard_map/ppermute | solution.py:29
  203.0 42.4 %collective-permute-start.23 = (bf16[64,7168]{1,0:T(8,128)(2,1)S(1)}, bf16[64,7168]{1,0:T(8,128)(2,1)S(1)}, u32[]{:S(2)}, u32[]{:S(2)}) collective-permute-start(bf16[64,7168]{1,0:T(8,128)(2,1)S(1)} %shard_map.144), channel_id=1, source_target_pairs={{0,112},{1,113},{2,114},{3,115},{4,116},{5,117},{6,118},{7,119},{8... | collective-permute-start | bytes 2752520 | tf_op jit(solution)/shard_map/ppermute | solution.py:29
  208.5 35.7 %collective-permute-start.19 = (bf16[32,7168]{1,0:T(8,128)(2,1)S(1)}, bf16[32,7168]{1,0:T(8,128)(2,1)S(1)}, u32[]{:S(2)}, u32[]{:S(2)}) collective-permute-start(bf16[32,7168]{1,0:T(8,128)(2,1)S(1)} %copy-done.21), channel_id=1, source_target_pairs={{0,2},{1,3},{2,0},{3,1},{4,6},{5,7},{6,4},{7,5},{8,10},{9,11},{10,... | collective-permute-start | bytes 1376264 | tf_op jit(solution)/shard_map/ppermute | solution.py:29
  214.7 39.3 %collective-permute-start.25 = (bf16[32,7168]{1,0:T(8,128)(2,1)S(1)}, bf16[32,7168]{1,0:T(8,128)(2,1)S(1)}, u32[]{:S(2)}, u32[]{:S(2)}) collective-permute-start(bf16[32,7168]{1,0:T(8,128)(2,1)S(1)} %copy-done.19), channel_id=1, source_target_pairs={{0,2},{1,3},{2,0},{3,1},{4,6},{5,7},{6,4},{7,5},{8,10},{9,11},{10,... | collective-permute-start | bytes 1376264 | tf_op jit(solution)/shard_map/ppermute | solution.py:29
  218.5 37.9 %collective-permute-start.17 = (bf16[32,7168]{1,0:T(8,128)(2,1)S(1)}, bf16[32,7168]{1,0:T(8,128)(2,1)S(1)}, u32[]{:S(2)}, u32[]{:S(2)}) collective-permute-start(bf16[32,7168]{1,0:T(8,128)(2,1)S(1)} %shard_map.139), channel_id=1, source_target_pairs={{0,8},{1,9},{2,10},{3,11},{4,12},{5,13},{6,14},{7,15},{8,0},{9,1},... | collective-permute-start | bytes 1376264 | tf_op jit(solution)/shard_map/ppermute | solution.py:29
  244.4 24.5 %collective-permute-start.20 = (bf16[32,7168]{1,0:T(8,128)(2,1)S(1)}, bf16[32,7168]{1,0:T(8,128)(2,1)S(1)}, u32[]{:S(2)}, u32[]{:S(2)}) collective-permute-start(bf16[32,7168]{1,0:T(8,128)(2,1)S(1)} %shard_map.141), channel_id=1, source_target_pairs={{0,16},{1,17},{2,18},{3,19},{4,20},{5,21},{6,22},{7,23},{8,24},{9,... | collective-permute-start | bytes 1376264 | tf_op jit(solution)/shard_map/ppermute | solution.py:29
  245.4 16.5 %collective-permute-start.24 = (bf16[32,7168]{1,0:T(8,128)(2,1)S(1)}, bf16[32,7168]{1,0:T(8,128)(2,1)S(1)}, u32[]{:S(2)}, u32[]{:S(2)}) collective-permute-start(bf16[32,7168]{1,0:T(8,128)(2,1)S(1)} %shard_map.145), channel_id=1, source_target_pairs={{0,112},{1,113},{2,114},{3,115},{4,116},{5,117},{6,118},{7,119},{8... | collective-permute-start | bytes 1376264 | tf_op jit(solution)/shard_map/ppermute | solution.py:29
  (33 other events, 300.1 us)
where the time goes:
time: 272 us; the launch traced here: 271 us
  waiting for transfers between devices  130 us (48%)
  starting transfers between devices  60.7 us (22%)
  Pallas kernels  57.9 us (21%)
  local copies, waits for them, and re-layouts  17.7 us (7%)
  other arithmetic  3.32 us (1%)
    ppermute x27, waiting for transfers between devices, move(): return lax.ppermute(block, ('pp', 'ep'), route)  103 us
    ppermute x27, starting transfers between devices, move(): return lax.ppermute(block, ('pp', 'ep'), route)  46.8 us
    pallas_call x2, Pallas kernels, through_expert(): pl.pallas_call(functools.partial(kernel, steps), grid=(2 * steps,), out_s...  38 us
    all_to_all x3, waiting for transfers between devices, along_y(): lax.all_to_all(rows.reshape(shape), 'ep', 0, 0, axis_index_groups=groups,...  27.6 us
    pallas_call x15, Pallas kernels, whole(): pl.pallas_call(kernel, out_shape=outs, in_specs=[pl.BlockSpec(memory_spac...  19.9 us
    unnamed x54, local copies, waits for them, and re-layouts  17.4 us
    all_to_all x3, starting transfers between devices, along_y(): lax.all_to_all(rows.reshape(shape), 'ep', 0, 0, axis_index_groups=groups,...  13.8 us
  transfers between devices with their start and end apart: 30, of which 17 were waited for; matrix products, arithmetic and copies ran while one was open for 1% of the time, Pallas kernels for 21%

commit v1 on v0

--- a/solution.py
+++ b/solution.py
@@ -11,6 +11,7 @@
 NY, NX, NC = 4, 2, 2
 ORDER = (1, 3, 2, 0)
 WIDE = 1024
+LANES = 128
 VMEM = pltpu.CompilerParams(vmem_limit_bytes=40 * 1024 * 1024)
 LIGHT = pl.CostEstimate(flops=1000, bytes_accessed=1000, transcendentals=0)
 
@@ -53,7 +54,7 @@
     return pl.pallas_call(
         kernel,
         out_shape=outs,
-        in_specs=[pl.BlockSpec(memory_space=pltpu.VMEM)] * len(operands),
+        in_specs=[pl.BlockSpec(memory_space=pltpu.SMEM if o.shape == (1,) else pltpu.VMEM) for o in operands],
         out_specs=jax.tree.map(lambda _: pl.BlockSpec(memory_space=pltpu.VMEM), outs),
         scratch_shapes=scratch,
         compiler_params=VMEM,
@@ -104,16 +105,23 @@
             pairs[(2 * e + 1) * cap : (2 * e + 2) * cap, here] = two[e * cap : (e + 1) * cap]
 
 
-def unpick_kernel(order, *refs):
+def unpick_kernel(*refs):
     *parts, out = refs
-    chosen = one_hot(order[...]).T
-    for j in range(0, out.shape[1], WIDE):
-        rows = jnp.concatenate([p[:, j : j + WIDE] for p in parts], axis=0)
-        out[:, j : j + WIDE] = dot(chosen, rows).astype(jnp.bfloat16)
-
-
-def unpick(order, parts):
-    return whole(unpick_kernel, table(order.shape[1], parts[0].shape[1]), order, *parts)
+    tokens, features = out.shape
+
+    def rows(here):
+        return jnp.concatenate([p[:, here] for p in parts], axis=0)
+
+    token = rows(slice(features, features + LANES)).astype(jnp.float32)
+    index = lax.broadcasted_iota(jnp.int32, (tokens, LANES), 1).astype(jnp.float32)
+    chosen = (token == index).astype(jnp.bfloat16).T
+    for j in range(0, features, WIDE):
+        here = slice(j, j + WIDE)
+        out[:, here] = dot(chosen, rows(here)).astype(jnp.bfloat16)
+
+
+def unpick(parts, tokens, features):
+    return whole(unpick_kernel, table(tokens, features), *parts)
 
 
 def sum_kernel(near, far, *outs):
@@ -133,20 +141,23 @@
     return sum(b[:, across].astype(jnp.float32) for b in blocks)
 
 
-def ahead_kernel(first, summed, kept, gates, *refs):
+def ahead_kernel(first, summed, kept, gates, tokens, *refs):
     *blocks, out = refs
-    here = slice(first, first + out.shape[0])
-    for j in range(0, out.shape[1], WIDE):
+    rows, features = out.shape[0], kept.shape[1]
+    here = slice(first, first + rows)
+    out[:, features:] = jnp.broadcast_to(tokens[here], (rows, LANES)).astype(jnp.bfloat16)
+    for j in range(0, features, WIDE):
         across = slice(j, j + WIDE)
         total = read_total(blocks, summed, across)
         out[:, across] = (kept[here, across].astype(jnp.float32) + gates[here] * total).astype(jnp.bfloat16)
 
 
-def back_kernel(first, summed, kept, cotangent, scales, gates, *refs):
+def back_kernel(first, summed, kept, gates, tokens, cotangent, scales, *refs):
     *blocks, out, grads = refs
-    rows, features = out.shape
+    rows, features = out.shape[0], kept.shape[1]
     here = slice(first, first + rows)
     scale = scales[here]
+    out[:, features:] = jnp.broadcast_to(tokens[here], (rows, LANES)).astype(jnp.bfloat16)
     inner_sum = jnp.zeros((rows, 1), jnp.float32)
     for j in range(0, features, WIDE):
         across = slice(j, j + WIDE)
@@ -322,12 +333,11 @@
     up_far = move(up_weight[0, 0], dc=1)
     down_far = move(down_weight[0, 0], dc=1)
     weights = (gate_weight[0, 0], gate_far, up_weight[0, 0], up_far, down_weight[0, 0], down_far)
-    ahead_places, back_places = move(ahead_turn, dpp=1), move(back_turn, dpp=-1)
 
     normed_ahead, ahead_kept, _ = norm(ahead_input[0], ahead_order, ahead_turn)
     ahead_near = along_y(normed_ahead)
     normed_back, back_kept, scales_back = norm(back_input[0], back_order, back_turn)
-    back_near = along_y(after(normed_back, ahead_near, far_cotangent, far_order, ahead_places, back_places))
+    back_near = along_y(after(normed_back, ahead_near, far_cotangent, far_order))
 
     ahead_far = cross(ahead_near)
     pairs, cotangent_kept = whole(
@@ -342,24 +352,24 @@
     back_far = cross(back_near, pairs, ahead_far)
     pairs = along_y(pairs)
 
-    groups = (2 * cap, cap, cap)
+    ahead_groups, back_groups = (2 * cap, 2 * cap), (2 * cap, cap, cap)
     wide = lambda dtype: pltpu.VMEM((2 * tokens, 2 * units), dtype)
     partials = through_expert(
         forward_kernel,
         place,
         (ahead_near, ahead_far),
         weights,
-        (*groups, *groups),
+        (*ahead_groups, *ahead_groups),
         False,
         [wide(jnp.float32)] * 2 + [wide(jnp.bfloat16)] * 2,
     )
-    ahead_home, ahead_away = partials[:3], partials[3:]
+    ahead_home, ahead_away = partials[:2], partials[2:]
     partials = through_expert(
         backward_kernel,
         after(place, *ahead_home),
         (back_near, back_far, pairs),
         weights,
-        (*groups, *groups),
+        (*back_groups, *back_groups),
         True,
         [wide(jnp.float32)] * 3 + [wide(jnp.bfloat16)] * 4,
     )
@@ -367,7 +377,7 @@
 
     def to_owner(home, other, *first):
         blocks = whole(sum_kernel, [table(cap, features)] * (home.shape[0] // cap), home, other)
-        return [move(b, dy=-k) for b, k in zip(blocks, first)]
+        return blocks[-1], [move(b, dy=-k) for b, k in zip(blocks, first)]
 
     def in_turn(turn, values):
         chosen = lax.broadcasted_iota(jnp.int32, (tokens, tokens), 0) == turn
@@ -376,45 +386,48 @@
     ahead_gates = in_turn(ahead_turn, ahead_gate)
     back_gates = in_turn(back_turn, back_gate)
 
+    token = jnp.arange(tokens, dtype=jnp.float32)[None]
+    ahead_rows = (ahead_kept, ahead_gates, in_turn(ahead_turn, token))
+    back_rows = (back_kept, back_gates, in_turn(back_turn, token), cotangent_kept, scales_back)
+
     def finish_ahead(first, blocks, summed=False):
         rows = cap if summed else cap * len(blocks)
         kernel = functools.partial(ahead_kernel, first * cap, summed)
-        return move(whole(kernel, table(rows, features), ahead_kept, ahead_gates, *blocks), dpp=1)
+        return whole(kernel, table(rows, features + LANES), *ahead_rows, *blocks)
 
     def finish_back(first, blocks, summed=False):
         rows = cap if summed else cap * len(blocks)
-        return move(
-            whole(
-                functools.partial(back_kernel, first * cap, summed),
-                table(rows, features),
-                back_kept,
-                cotangent_kept,
-                scales_back,
-                back_gates,
-                *blocks,
-                scratch=[pltpu.VMEM((rows, features), jnp.float32)],
-            ),
-            dpp=-1,
+        return whole(
+            functools.partial(back_kernel, first * cap, summed),
+            table(rows, features + LANES),
+            *back_rows,
+            *blocks,
+            scratch=[pltpu.VMEM((rows, features), jnp.float32)],
         )
 
-    ahead_0 = cross(ahead_away[0], pairs)
-    back_0 = cross(back_away[0])
-    ahead_sums = to_owner(after(ahead_home[0], back_home[0]), ahead_0, *ORDER[:2])
-    back_1 = cross(back_away[1], ahead_0)
-    back_sums = to_owner(back_home[0], back_0, *ORDER[:2])
-    ahead_1 = cross(ahead_away[1], back_0, *ahead_sums)
-    ahead_low = finish_ahead(0, ahead_sums)
-    ahead_2 = cross(ahead_away[2], back_1)
-    back_sum = to_owner(back_home[1], back_1, *ORDER[2:3])
-    back_low = finish_back(0, back_sums)
-    back_2 = cross(back_away[2], ahead_1, *back_sums)
-    ahead_sum = to_owner(after(ahead_home[1], *back_sum), ahead_1, *ORDER[2:3])
-    back_middle = finish_back(2, [after(back_sum[0], ahead_low)])
-    ahead_middle = finish_ahead(2, [after(ahead_sum[0], ahead_low)])
-    ahead_last = finish_ahead(3, [ahead_home[2], ahead_2], True)
-    back_last = finish_back(3, [after(back_home[2], back_low), back_2], True)
-    ahead_output = unpick(ahead_places, [ahead_low, ahead_middle, ahead_last])
-    back_gradient = unpick(back_places, [back_low, back_middle, back_last])
+
+    a0 = cross(ahead_away[0])
+    b0 = cross(back_away[0], a0)
+    b1 = cross(back_away[1])
+    done, asum = to_owner(after(ahead_home[0], back_home[0]), a0, *ORDER[:2])
+    done, bsum = to_owner(after(back_home[0], done), b0, *ORDER[:2])
+    done, bsum2 = to_owner(after(back_home[1], done), b1, *ORDER[2:3])
+    a1 = cross(ahead_away[1], b0, b1)
+    ahead_low = finish_ahead(0, [after(asum[0], done), asum[1]])
+    zA13 = move(ahead_low, dpp=1)
+    back_low = finish_back(0, [after(bsum[0], ahead_low), bsum[1]])
+    zB13 = move(back_low, dpp=-1)
+    b2 = cross(back_away[2], b1)
+    done = finish_back(2, [after(bsum2[0], back_low)])
+    zB2 = move(done, dpp=-1)
+    ahead_sum, ahead_own = whole(sum_kernel, [table(cap, features)] * 2, after(ahead_home[1], done), a1)
+    asum2 = [move(ahead_sum, dy=-ORDER[2])]
+    done = finish_back(3, [after(back_home[2], ahead_own, zB13), b2], True)
+    zB0 = move(done, dpp=-1)
+    done = finish_ahead(2, [after(asum2[0], done, zA13, b2), ahead_own])
+    zA2 = move(done, dpp=1)
+    ahead_output = unpick([after(zA13, done), zA2], tokens, features)
+    back_gradient = unpick([zB13, zB2, zB0], tokens, features)
     return (ahead_output[None], back_gradient[None])
 
 

time: 272 us -> 265 us (0.974)
  waiting for transfers between devices: 130 us -> 116 us
  local copies, waits for them, and re-layouts: 17.7 us -> 20.7 us
    all_to_all x3, waiting for transfers between devices: 27.6 us -> 19.8 us  [along_y(): lax.all_to_all(rows.reshape(shape), 'ep', 0, 0, axis_index_groups=groups,...]
    ppermute x27 -> x23, waiting for transfers between devices: 103 us -> 96.4 us  [move(): return lax.ppermute(block, ('pp', 'ep'), route)]
    unnamed x54 -> x50, local copies, waits for them, and re-layouts: 17.4 us -> 20.1 us
    pallas_call x15 -> x14, Pallas kernels: 19.9 us -> 22.3 us  [whole(): pl.pallas_call(kernel, out_shape=outs, in_specs=[pl.BlockSpec(memory_spac...]
    ppermute x27 -> x23, starting transfers between devices: 46.8 us -> 47.7 us  [move(): return lax.ppermute(block, ('pp', 'ep'), route)]
  transfers between devices with their start and end apart: 30 -> 26, of which waited for: 17 -> 12; matrix products, arithmetic and copies ran while one was open for 1% -> 1% of each run, Pallas kernels for 21% -> 22%
where the time goes in v1:
time: 265 us; the launch traced here: 263 us
  waiting for transfers between devices  116 us (44%)
  starting transfers between devices  61.7 us (23%)
  Pallas kernels  60.3 us (23%)
  local copies, waits for them, and re-layouts  20.7 us (8%)
  other arithmetic  3.4 us (1%)
    ppermute x23, waiting for transfers between devices, move(): return lax.ppermute(block, ('pp', 'ep'), route)  96.4 us
    ppermute x23, starting transfers between devices, move(): return lax.ppermute(block, ('pp', 'ep'), route)  47.7 us
    pallas_call x2, Pallas kernels, through_expert(): pl.pallas_call(functools.partial(kernel, steps), grid=(2 * steps,), out_s...  38.1 us
    pallas_call x14, Pallas kernels, whole(): pl.pallas_call(kernel, out_shape=outs, in_specs=[pl.BlockSpec(memory_spac...  22.3 us
    unnamed x50, local copies, waits for them, and re-layouts  20.1 us
    all_to_all x3, waiting for transfers between devices, along_y(): lax.all_to_all(rows.reshape(shape), 'ep', 0, 0, axis_index_groups=groups,...  19.8 us
    all_to_all x3, starting transfers between devices, along_y(): lax.all_to_all(rows.reshape(shape), 'ep', 0, 0, axis_index_groups=groups,...  14 us
  transfers between devices with their start and end apart: 26, of which 12 were waited for; matrix products, arithmetic and copies ran while one was open for 1% of the time, Pallas kernels for 22%

profile of v1, /device:TPU:0, one launch (start us, length us, event | category | flops | bytes accessed | tf_op | source)
XLA Modules:
  0.0 263.3 jit_solution(5385723801644412605)
XLA Ops:
  0.6 3.2 %collective-permute-start.4 = (bf16[128,7168]{1,0:T(8,128)(2,1)}, bf16[128,7168]{1,0:T(8,128)(2,1)}, u32[]{:S(2)}, u32[]{:S(2)}) collective-permute-start(bf16[128,7168]{1,0:T(8,128)(2,1)} %bitcast.31), channel_id=1, source_target_pairs={{0,2},{1,3},{2,0},{3,1},{4,6},{5,7},{6,4},{7,5},{8,10},{9,11},{10,... | collective-permute-start | bytes 5505032 | tf_op jit(solution)/shard_map/ppermute | solution.py:30
  11.8 4.6 %all-to-all-start = ((bf16[4,32,7168]{2,1,0:T(8,128)(2,1)}), bf16[4,32,7168]{2,1,0:T(8,128)(2,1)}, u32[]{:S(2)}, u32[]{:S(2)}) async-start(bf16[4,32,7168]{2,1,0:T(8,128)(2,1)} %bitcast.7), calls=%async_computation | async-start | bytes 3670016 | tf_op jit(solution)/shard_map/all_to_all | solution.py:314
  22.4 21.8 %collective-permute-done.5.far_order = s32[1,128]{1,0:T(1,128)S(1)} collective-permute-done((s32[1,128]{1,0:T(1,128)S(1)}, s32[1,128]{1,0:T(1,128)S(1)}, u32[]{:S(2)}, u32[]{:S(2)}) %collective-permute-start.5) | collective-permute-done | bytes 544 | tf_op jit(solution)/shard_map/ppermute | solution.py:30
  44.2 4.7 %all-to-all-start.1 = ((bf16[4,32,7168]{2,1,0:T(8,128)(2,1)}), bf16[4,32,7168]{2,1,0:T(8,128)(2,1)}, u32[]{:S(2)}, u32[]{:S(2)}) async-start(bf16[4,32,7168]{2,1,0:T(8,128)(2,1)} %bitcast.33), calls=%async_computation.1 | async-start | bytes 3670016 | tf_op jit(solution)/shard_map/all_to_all | solution.py:314
  51.9 19.8 %all-to-all-done.1 = bf16[4,32,7168]{2,1,0:T(8,128)(2,1)} async-done(((bf16[4,32,7168]{2,1,0:T(8,128)(2,1)}), bf16[4,32,7168]{2,1,0:T(8,128)(2,1)}, u32[]{:S(2)}, u32[]{:S(2)}) %all-to-all-start.1) | async-done | bytes 1835040 | tf_op jit(solution)/shard_map/all_to_all | solution.py:314
  79.3 4.7 %all-to-all-start.2 = ((bf16[4,64,7168]{2,1,0:T(8,128)(2,1)}), bf16[4,64,7168]{2,1,0:T(8,128)(2,1)}, u32[]{:S(2)}, u32[]{:S(2)}) async-start(bf16[4,64,7168]{2,1,0:T(8,128)(2,1)} %bitcast.30), calls=%async_computation.2 | async-start | bytes 7340032 | tf_op jit(solution)/shard_map/all_to_all | solution.py:314
  84.1 7.3 %collective-permute-done.far = bf16[128,7168]{1,0:T(8,128)(2,1)} collective-permute-done((bf16[128,7168]{1,0:T(8,128)(2,1)}, bf16[128,7168]{1,0:T(8,128)(2,1)}, u32[]{:S(2)}, u32[]{:S(2)}) %collective-permute-start) | collective-permute-done | bytes 1835040 | tf_op jit(solution)/shard_map/ppermute | solution.py:30
  91.3 3.2 %collective-permute-start.6 = (bf16[128,7168]{1,0:T(8,128)(2,1)}, bf16[128,7168]{1,0:T(8,128)(2,1)S(1)}, u32[]{:S(2)}, u32[]{:S(2)}) collective-permute-start(bf16[128,7168]{1,0:T(8,128)(2,1)} %bitcast.17.near), channel_id=1, source_target_pairs={{0,2},{1,3},{2,0},{3,1},{4,6},{5,7},{6,4},{7,5},{8,10},{9,11},{10,... | collective-permute-start | bytes 5505032 | tf_op jit(solution)/shard_map/ppermute | solution.py:30
  96.6 16.6 %shard_map.132 = (bf16[64,7168]{1,0:T(8,128)(2,1)S(1)}, bf16[64,7168]{1,0:T(8,128)(2,1)S(1)}, bf16[64,7168]{1,0:T(8,128)(2,1)}, bf16[64,7168]{1,0:T(8,128)(2,1)}) custom-call(s32[1]{0:T(128)} %bitcast.6.place, bf16[128,7168]{1,0:T(8,128)(2,1)} %bitcast.8.near, bf16[128,7168]{1,0:T(8,128)(2,1)} %collective-permute-done.far, bf16[7168,256]{1,0:T(8,128)(2,1)S(1)} %bitcast.29, ...), custom_call_target="tpu_custom_call" | custom-call | flops 1000 | bytes 1000 | tf_op jit(solution)/shard_map/pallas_call | solution.py:274
  114.4 21.6 %collective-permute-done.6.far = bf16[128,7168]{1,0:T(8,128)(2,1)S(1)} collective-permute-done((bf16[128,7168]{1,0:T(8,128)(2,1)}, bf16[128,7168]{1,0:T(8,128)(2,1)S(1)}, u32[]{:S(2)}, u32[]{:S(2)}) %collective-permute-start.6) | collective-permute-done | bytes 1835040 | tf_op jit(solution)/shard_map/ppermute | solution.py:30
  138.8 21.5 %shard_map.135 = (bf16[64,7168]{1,0:T(8,128)(2,1)S(1)}, bf16[32,7168]{1,0:T(8,128)(2,1)S(1)}, bf16[32,7168]{1,0:T(8,128)(2,1)S(1)}, bf16[64,7168]{1,0:T(8,128)(2...) custom-call(s32[1]{0:T(128)} %bitcast.6.place, bf16[128,7168]{1,0:T(8,128)(2,1)} %bitcast.17.near, ...), custom_call_target="tpu_custom_call" | custom-call | flops 1000 | bytes 1000 | tf_op jit(solution)/shard_map/pallas_call | solution.py:274
  160.3 3.3 %collective-permute-start.9 = (bf16[64,7168]{1,0:T(8,128)(2,1)S(1)}, bf16[64,7168]{1,0:T(8,128)(2,1)S(1)}, u32[]{:S(2)}, u32[]{:S(2)}) collective-permute-start(bf16[64,7168]{1,0:T(8,128)(2,1)S(1)} %get-tuple-element.64), channel_id=1, source_target_pairs={{0,2},{1,3},{2,0},{3,1},{4,6},{5,7},{6,4},{7,5},{8,10},{9,11},{10,... | collective-permute-start | bytes 2752520 | tf_op jit(solution)/shard_map/ppermute | solution.py:30
  166.1 3.2 %collective-permute-start.8 = (bf16[32,7168]{1,0:T(8,128)(2,1)}, bf16[32,7168]{1,0:T(8,128)(2,1)}, u32[]{:S(2)}, u32[]{:S(2)}) collective-permute-start(bf16[32,7168]{1,0:T(8,128)(2,1)} %get-tuple-element.59), channel_id=1, source_target_pairs={{0,12},{1,13},{2,14},{3,15},{4,0},{5,1},{6,2},{7,3},{8,4},{9,5},{1... | collective-permute-start | bytes 1376264 | tf_op jit(solution)/shard_map/ppermute | solution.py:30
  169.4 13.8 %collective-permute-done.9.far = bf16[64,7168]{1,0:T(8,128)(2,1)S(1)} collective-permute-done((bf16[64,7168]{1,0:T(8,128)(2,1)S(1)}, bf16[64,7168]{1,0:T(8,128)(2,1)S(1)}, u32[]{:S(2)}, u32[]{:S(2)}) %collective-permute-start.9) | collective-permute-done | bytes 917536 | tf_op jit(solution)/shard_map/ppermute | solution.py:30
  190.5 3.2 %collective-permute-start.16 = (bf16[64,7168]{1,0:T(8,128)(2,1)}, bf16[64,7168]{1,0:T(8,128)(2,1)}, u32[]{:S(2)}, u32[]{:S(2)}) collective-permute-start(bf16[64,7168]{1,0:T(8,128)(2,1)} %get-tuple-element.77), channel_id=1, source_target_pairs={{0,2},{1,3},{2,0},{3,1},{4,6},{5,7},{6,4},{7,5},{8,10},{9,11},{10,... | collective-permute-start | bytes 2752520 | tf_op jit(solution)/shard_map/ppermute | solution.py:30
  202.7 4.1 %collective-permute-start.18 = (bf16[64,7296]{1,0:T(8,128)(2,1)S(1)}, bf16[64,7296]{1,0:T(8,128)(2,1)S(1)}, u32[]{:S(2)}, u32[]{:S(2)}) collective-permute-start(bf16[64,7296]{1,0:T(8,128)(2,1)S(1)} %shard_map.140), channel_id=1, source_target_pairs={{0,112},{1,113},{2,114},{3,115},{4,116},{5,117},{6,118},{7,119},{8... | collective-permute-start | bytes 2801672 | tf_op jit(solution)/shard_map/ppermute | solution.py:30
  206.9 3.2 %collective-permute-start.13 = (bf16[32,7168]{1,0:T(8,128)(2,1)S(1)}, bf16[32,7168]{1,0:T(8,128)(2,1)S(1)}, u32[]{:S(2)}, u32[]{:S(2)}) collective-permute-start(bf16[32,7168]{1,0:T(8,128)(2,1)S(1)} %shard_map.138), channel_id=1, source_target_pairs={{0,8},{1,9},{2,10},{3,11},{4,12},{5,13},{6,14},{7,15},{8,0},{9,1},... | collective-permute-start | bytes 1376264 | tf_op jit(solution)/shard_map/ppermute | solution.py:30
  212.0 8.7 %collective-permute-done.13.refs_0_ = bf16[32,7168]{1,0:T(8,128)(2,1)S(1)} collective-permute-done((bf16[32,7168]{1,0:T(8,128)(2,1)S(1)}, bf16[32,7168]{1,0:T(8,128)(2,1)S(1)}, u32[]{:S(2)}, u32[]{:S(2)}) %collective-permute-start.13) | collective-permute-done | bytes 458784 | tf_op jit(solution)/shard_map/ppermute | solution.py:30
  223.0 4.1 %collective-permute-start.17 = (bf16[32,7168]{1,0:T(8,128)(2,1)S(1)}, bf16[32,7168]{1,0:T(8,128)(2,1)S(1)}, u32[]{:S(2)}, u32[]{:S(2)}) collective-permute-start(bf16[32,7168]{1,0:T(8,128)(2,1)S(1)} %get-tuple-element.78), channel_id=1, source_target_pairs={{0,8},{1,9},{2,10},{3,11},{4,12},{5,13},{6,14},{7,15},{8,0},{9,1},... | collective-permute-start | bytes 1376264 | tf_op jit(solution)/shard_map/ppermute | solution.py:30
  227.0 4.9 %collective-permute-done.18.refs_0_ = bf16[64,7296]{1,0:T(8,128)(2,1)S(1)} collective-permute-done((bf16[64,7296]{1,0:T(8,128)(2,1)S(1)}, bf16[64,7296]{1,0:T(8,128)(2,1)S(1)}, u32[]{:S(2)}, u32[]{:S(2)}) %collective-permute-start.18) | collective-permute-done | bytes 933920 | tf_op jit(solution)/shard_map/ppermute | solution.py:30
  231.9 5.7 %collective-permute-done.19.refs_1_ = bf16[32,7168]{1,0:T(8,128)(2,1)S(1)} collective-permute-done((bf16[32,7168]{1,0:T(8,128)(2,1)S(1)}, bf16[32,7168]{1,0:T(8,128)(2,1)S(1)}, u32[]{:S(2)}, u32[]{:S(2)}) %collective-permute-start.19) | collective-permute-done | bytes 458784 | tf_op jit(solution)/shard_map/ppermute | solution.py:30
  238.9 8.6 %collective-permute-start.21 = (bf16[32,7296]{1,0:T(8,128)(2,1)S(1)}, bf16[32,7296]{1,0:T(8,128)(2,1)S(1)}, u32[]{:S(2)}, u32[]{:S(2)}) collective-permute-start(bf16[32,7296]{1,0:T(8,128)(2,1)S(1)} %shard_map.141), channel_id=1, source_target_pairs={{0,112},{1,113},{2,114},{3,115},{4,116},{5,117},{6,118},{7,119},{8... | collective-permute-start | bytes 1400840 | tf_op jit(solution)/shard_map/ppermute | solution.py:30
  249.4 4.1 %collective-permute-done.21.refs_1_ = bf16[32,7296]{1,0:T(8,128)(2,1)S(1)} collective-permute-done((bf16[32,7296]{1,0:T(8,128)(2,1)S(1)}, bf16[32,7296]{1,0:T(8,128)(2,1)S(1)}, u32[]{:S(2)}, u32[]{:S(2)}) %collective-permute-start.21) | collective-permute-done | bytes 466976 | tf_op jit(solution)/shard_map/ppermute | solution.py:30
  253.6 5.0 %collective-permute-done.22.refs_2_ = bf16[32,7296]{1,0:T(8,128)(2,1)S(1)} collective-permute-done((bf16[32,7296]{1,0:T(8,128)(2,1)S(1)}, bf16[32,7296]{1,0:T(8,128)(2,1)S(1)}, u32[]{:S(2)}, u32[]{:S(2)}) %collective-permute-start.22) | collective-permute-done | bytes 466976 | tf_op jit(solution)/shard_map/ppermute | solution.py:30
  (113 shorter events, 61.5 us)
Async XLA Ops:
  0.6 43.5 %collective-permute-start.4 = (bf16[128,7168]{1,0:T(8,128)(2,1)}, bf16[128,7168]{1,0:T(8,128)(2,1)}, u32[]{:S(2)}, u32[]{:S(2)}) collective-permute-start(bf16[128,7168]{1,0:T(8,128)(2,1)} %bitcast.31), channel_id=1, source_target_pairs={{0,2},{1,3},{2,0},{3,1},{4,6},{5,7},{6,4},{7,5},{8,10},{9,11},{10,... | collective-permute-start | bytes 5505032 | tf_op jit(solution)/shard_map/ppermute | solution.py:30
  11.8 32.3 %all-to-all-start = ((bf16[4,32,7168]{2,1,0:T(8,128)(2,1)}), bf16[4,32,7168]{2,1,0:T(8,128)(2,1)}, u32[]{:S(2)}, u32[]{:S(2)}) async-start(bf16[4,32,7168]{2,1,0:T(8,128)(2,1)} %bitcast.7), calls=%async_computation | async-start | bytes 3670016 | tf_op jit(solution)/shard_map/all_to_all | solution.py:314
  16.4 27.7 %collective-permute-start.5 = (s32[1,128]{1,0:T(1,128)S(1)}, s32[1,128]{1,0:T(1,128)S(1)}, u32[]{:S(2)}, u32[]{:S(2)}) collective-permute-start(s32[1,128]{1,0:T(1,128)S(1)} %multiply_add_fusion.expert_order.near_order), channel_id=1, source_target_pairs={{0,2},{1,3},{2,0},{3,1},{4,6},{5,7},{6,4},{7,5},{8,10},{9,11},{10,... | collective-permute-start | bytes 1544 | tf_op jit(solution)/shard_map/ppermute | solution.py:30
  17.0 77.6 %collective-permute-start.1 = (bf16[7168,256]{1,0:T(8,128)(2,1)}, bf16[7168,256]{1,0:T(8,128)(2,1)}, u32[]{:S(2)}, u32[]{:S(2)}) collective-permute-start(bf16[7168,256]{1,0:T(8,128)(2,1)} %bitcast.27), channel_id=1, source_target_pairs={{0,1},{1,0},{2,3},{3,2},{4,5},{5,4},{6,7},{7,6},{8,9},{9,8},{10,11... | collective-permute-start | bytes 11010056 | tf_op jit(solution)/shard_map/ppermute | solution.py:30
  17.0 77.6 %collective-permute-start.2 = (bf16[7168,256]{1,0:T(8,128)(2,1)}, bf16[7168,256]{1,0:T(8,128)(2,1)}, u32[]{:S(2)}, u32[]{:S(2)}) collective-permute-start(bf16[7168,256]{1,0:T(8,128)(2,1)} %bitcast.39), channel_id=1, source_target_pairs={{0,1},{1,0},{2,3},{3,2},{4,5},{5,4},{6,7},{7,6},{8,9},{9,8},{10,11... | collective-permute-start | bytes 11010056 | tf_op jit(solution)/shard_map/ppermute | solution.py:30
  17.5 77.0 %collective-permute-start.3 = (bf16[256,7168]{1,0:T(8,128)(2,1)}, bf16[256,7168]{1,0:T(8,128)(2,1)}, u32[]{:S(2)}, u32[]{:S(2)}) collective-permute-start(bf16[256,7168]{1,0:T(8,128)(2,1)} %bitcast.42), channel_id=1, source_target_pairs={{0,1},{1,0},{2,3},{3,2},{4,5},{5,4},{6,7},{7,6},{8,9},{9,8},{10,11... | collective-permute-start | bytes 11010056 | tf_op jit(solution)/shard_map/ppermute | solution.py:30
  44.2 27.5 %all-to-all-start.1 = ((bf16[4,32,7168]{2,1,0:T(8,128)(2,1)}), bf16[4,32,7168]{2,1,0:T(8,128)(2,1)}, u32[]{:S(2)}, u32[]{:S(2)}) async-start(bf16[4,32,7168]{2,1,0:T(8,128)(2,1)} %bitcast.33), calls=%async_computation.1 | async-start | bytes 3670016 | tf_op jit(solution)/shard_map/all_to_all | solution.py:314
  48.8 42.5 %collective-permute-start = (bf16[128,7168]{1,0:T(8,128)(2,1)}, bf16[128,7168]{1,0:T(8,128)(2,1)}, u32[]{:S(2)}, u32[]{:S(2)}) collective-permute-start(bf16[128,7168]{1,0:T(8,128)(2,1)} %bitcast.8.near), channel_id=1, source_target_pairs={{0,2},{1,3},{2,0},{3,1},{4,6},{5,7},{6,4},{7,5},{8,10},{9,11},{10,... | collective-permute-start | bytes 5505032 | tf_op jit(solution)/shard_map/ppermute | solution.py:30
  79.3 58.0 %all-to-all-start.2 = ((bf16[4,64,7168]{2,1,0:T(8,128)(2,1)}), bf16[4,64,7168]{2,1,0:T(8,128)(2,1)}, u32[]{:S(2)}, u32[]{:S(2)}) async-start(bf16[4,64,7168]{2,1,0:T(8,128)(2,1)} %bitcast.30), calls=%async_computation.2 | async-start | bytes 7340032 | tf_op jit(solution)/shard_map/all_to_all | solution.py:314
  91.3 44.7 %collective-permute-start.6 = (bf16[128,7168]{1,0:T(8,128)(2,1)}, bf16[128,7168]{1,0:T(8,128)(2,1)S(1)}, u32[]{:S(2)}, u32[]{:S(2)}) collective-permute-start(bf16[128,7168]{1,0:T(8,128)(2,1)} %bitcast.17.near), channel_id=1, source_target_pairs={{0,2},{1,3},{2,0},{3,1},{4,6},{5,7},{6,4},{7,5},{8,10},{9,11},{10,... | collective-permute-start | bytes 5505032 | tf_op jit(solution)/shard_map/ppermute | solution.py:30
  114.2 46.1 %collective-permute-start.7 = (bf16[64,7168]{1,0:T(8,128)(2,1)}, bf16[64,7168]{1,0:T(8,128)(2,1)}, u32[]{:S(2)}, u32[]{:S(2)}) collective-permute-start(bf16[64,7168]{1,0:T(8,128)(2,1)} %get-tuple-element.58), channel_id=1, source_target_pairs={{0,2},{1,3},{2,0},{3,1},{4,6},{5,7},{6,4},{7,5},{8,10},{9,11},{10,... | collective-permute-start | bytes 2752520 | tf_op jit(solution)/shard_map/ppermute | solution.py:30
  160.3 22.9 %collective-permute-start.9 = (bf16[64,7168]{1,0:T(8,128)(2,1)S(1)}, bf16[64,7168]{1,0:T(8,128)(2,1)S(1)}, u32[]{:S(2)}, u32[]{:S(2)}) collective-permute-start(bf16[64,7168]{1,0:T(8,128)(2,1)S(1)} %get-tuple-element.64), channel_id=1, source_target_pairs={{0,2},{1,3},{2,0},{3,1},{4,6},{5,7},{6,4},{7,5},{8,10},{9,11},{10,... | collective-permute-start | bytes 2752520 | tf_op jit(solution)/shard_map/ppermute | solution.py:30
  163.6 26.1 %collective-permute-start.10 = (bf16[32,7168]{1,0:T(8,128)(2,1)S(1)}, bf16[32,7168]{1,0:T(8,128)(2,1)S(1)}, u32[]{:S(2)}, u32[]{:S(2)}) collective-permute-start(bf16[32,7168]{1,0:T(8,128)(2,1)S(1)} %get-tuple-element.67), channel_id=1, source_target_pairs={{0,2},{1,3},{2,0},{3,1},{4,6},{5,7},{6,4},{7,5},{8,10},{9,11},{10,... | collective-permute-start | bytes 1376264 | tf_op jit(solution)/shard_map/ppermute | solution.py:30
  166.1 30.5 %collective-permute-start.8 = (bf16[32,7168]{1,0:T(8,128)(2,1)}, bf16[32,7168]{1,0:T(8,128)(2,1)}, u32[]{:S(2)}, u32[]{:S(2)}) collective-permute-start(bf16[32,7168]{1,0:T(8,128)(2,1)} %get-tuple-element.59), channel_id=1, source_target_pairs={{0,12},{1,13},{2,14},{3,15},{4,0},{5,1},{6,2},{7,3},{8,4},{9,5},{1... | collective-permute-start | bytes 1376264 | tf_op jit(solution)/shard_map/ppermute | solution.py:30
  169.4 27.3 %collective-permute-start.11 = (bf16[32,7168]{1,0:T(8,128)(2,1)}, bf16[32,7168]{1,0:T(8,128)(2,1)}, u32[]{:S(2)}, u32[]{:S(2)}) collective-permute-start(bf16[32,7168]{1,0:T(8,128)(2,1)} %get-tuple-element.61), channel_id=1, source_target_pairs={{0,4},{1,5},{2,6},{3,7},{4,8},{5,9},{6,10},{7,11},{8,12},{9,13},{1... | collective-permute-start | bytes 1376264 | tf_op jit(solution)/shard_map/ppermute | solution.py:30
  184.2 15.5 %collective-permute-start.14 = (bf16[32,7168]{1,0:T(8,128)(2,1)}, bf16[32,7168]{1,0:T(8,128)(2,1)}, u32[]{:S(2)}, u32[]{:S(2)}) collective-permute-start(bf16[32,7168]{1,0:T(8,128)(2,1)} %get-tuple-element.72), channel_id=1, source_target_pairs={{0,12},{1,13},{2,14},{3,15},{4,0},{5,1},{6,2},{7,3},{8,4},{9,5},{1... | collective-permute-start | bytes 1376264 | tf_op jit(solution)/shard_map/ppermute | solution.py:30
  190.5 31.0 %collective-permute-start.16 = (bf16[64,7168]{1,0:T(8,128)(2,1)}, bf16[64,7168]{1,0:T(8,128)(2,1)}, u32[]{:S(2)}, u32[]{:S(2)}) collective-permute-start(bf16[64,7168]{1,0:T(8,128)(2,1)} %get-tuple-element.77), channel_id=1, source_target_pairs={{0,2},{1,3},{2,0},{3,1},{4,6},{5,7},{6,4},{7,5},{8,10},{9,11},{10,... | collective-permute-start | bytes 2752520 | tf_op jit(solution)/shard_map/ppermute | solution.py:30
  202.7 29.2 %collective-permute-start.18 = (bf16[64,7296]{1,0:T(8,128)(2,1)S(1)}, bf16[64,7296]{1,0:T(8,128)(2,1)S(1)}, u32[]{:S(2)}, u32[]{:S(2)}) collective-permute-start(bf16[64,7296]{1,0:T(8,128)(2,1)S(1)} %shard_map.140), channel_id=1, source_target_pairs={{0,112},{1,113},{2,114},{3,115},{4,116},{5,117},{6,118},{7,119},{8... | collective-permute-start | bytes 2801672 | tf_op jit(solution)/shard_map/ppermute | solution.py:30
  206.8 31.6 %collective-permute-start.12 = (bf16[64,7296]{1,0:T(8,128)(2,1)S(1)}, bf16[64,7296]{1,0:T(8,128)(2,1)S(1)}, u32[]{:S(2)}, u32[]{:S(2)}) collective-permute-start(bf16[64,7296]{1,0:T(8,128)(2,1)S(1)} %shard_map.139), channel_id=1, source_target_pairs={{0,16},{1,17},{2,18},{3,19},{4,20},{5,21},{6,22},{7,23},{8,24},{9,... | collective-permute-start | bytes 2801672 | tf_op jit(solution)/shard_map/ppermute | solution.py:30
  206.9 13.9 %collective-permute-start.13 = (bf16[32,7168]{1,0:T(8,128)(2,1)S(1)}, bf16[32,7168]{1,0:T(8,128)(2,1)S(1)}, u32[]{:S(2)}, u32[]{:S(2)}) collective-permute-start(bf16[32,7168]{1,0:T(8,128)(2,1)S(1)} %shard_map.138), channel_id=1, source_target_pairs={{0,8},{1,9},{2,10},{3,11},{4,12},{5,13},{6,14},{7,15},{8,0},{9,1},... | collective-permute-start | bytes 1376264 | tf_op jit(solution)/shard_map/ppermute | solution.py:30
  210.0 27.6 %collective-permute-start.19 = (bf16[32,7168]{1,0:T(8,128)(2,1)S(1)}, bf16[32,7168]{1,0:T(8,128)(2,1)S(1)}, u32[]{:S(2)}, u32[]{:S(2)}) collective-permute-start(bf16[32,7168]{1,0:T(8,128)(2,1)S(1)} %copy-done.20), channel_id=1, source_target_pairs={{0,2},{1,3},{2,0},{3,1},{4,6},{5,7},{6,4},{7,5},{8,10},{9,11},{10,... | collective-permute-start | bytes 1376264 | tf_op jit(solution)/shard_map/ppermute | solution.py:30
  223.0 15.5 %collective-permute-start.17 = (bf16[32,7168]{1,0:T(8,128)(2,1)S(1)}, bf16[32,7168]{1,0:T(8,128)(2,1)S(1)}, u32[]{:S(2)}, u32[]{:S(2)}) collective-permute-start(bf16[32,7168]{1,0:T(8,128)(2,1)S(1)} %get-tuple-element.78), channel_id=1, source_target_pairs={{0,8},{1,9},{2,10},{3,11},{4,12},{5,13},{6,14},{7,15},{8,0},{9,1},... | collective-permute-start | bytes 1376264 | tf_op jit(solution)/shard_map/ppermute | solution.py:30
  238.8 22.6 %collective-permute-start.20 = (bf16[64,7296]{1,0:T(8,128)(2,1)S(1)}, bf16[64,7296]{1,0:T(8,128)(2,1)S(1)}, u32[]{:S(2)}, u32[]{:S(2)}) collective-permute-start(bf16[64,7296]{1,0:T(8,128)(2,1)S(1)} %shard_map.144), channel_id=1, source_target_pairs={{0,16},{1,17},{2,18},{3,19},{4,20},{5,21},{6,22},{7,23},{8,24},{9,... | collective-permute-start | bytes 2801672 | tf_op jit(solution)/shard_map/ppermute | solution.py:30
  238.9 14.7 %collective-permute-start.21 = (bf16[32,7296]{1,0:T(8,128)(2,1)S(1)}, bf16[32,7296]{1,0:T(8,128)(2,1)S(1)}, u32[]{:S(2)}, u32[]{:S(2)}) collective-permute-start(bf16[32,7296]{1,0:T(8,128)(2,1)S(1)} %shard_map.141), channel_id=1, source_target_pairs={{0,112},{1,113},{2,114},{3,115},{4,116},{5,117},{6,118},{7,119},{8... | collective-permute-start | bytes 1400840 | tf_op jit(solution)/shard_map/ppermute | solution.py:30
  (27 other events, 204.6 us)

commit v2 on v1

--- a/solution.py
+++ b/solution.py
@@ -11,6 +11,7 @@
 NY, NX, NC = 4, 2, 2
 ORDER = (1, 3, 2, 0)
 WIDE = 1024
+SPAN = 3584
 LANES = 128
 VMEM = pltpu.CompilerParams(vmem_limit_bytes=40 * 1024 * 1024)
 LIGHT = pl.CostEstimate(flops=1000, bytes_accessed=1000, transcendentals=0)
@@ -265,21 +266,21 @@
 
 def through_expert(kernel, place, rows, weights, parts, twice, scratch):
     features = rows[0].shape[1]
-    steps = features // WIDE
+    steps = features // SPAN
     first = lambda i: jnp.minimum(i, steps - 1)
     second = lambda i: jnp.maximum(i - steps, 0)
     both = lambda i: i % steps
-    gate = [pl.BlockSpec((WIDE, w.shape[1]), lambda i: ((both if twice else first)(i), 0)) for w in weights[:4]]
-    down = [pl.BlockSpec((w.shape[0], WIDE), lambda i: (0, (first if twice else second)(i))) for w in weights[4:]]
+    gate = [pl.BlockSpec((SPAN, w.shape[1]), lambda i: ((both if twice else first)(i), 0)) for w in weights[:4]]
+    down = [pl.BlockSpec((w.shape[0], SPAN), lambda i: (0, (first if twice else second)(i))) for w in weights[4:]]
     return pl.pallas_call(
         functools.partial(kernel, steps),
         grid=(2 * steps,),
         out_shape=[table(n, features) for n in parts],
         in_specs=[pl.BlockSpec(memory_space=pltpu.SMEM)]
-        + [pl.BlockSpec((r.shape[0], WIDE), lambda i: (0, first(i))) for r in rows]
+        + [pl.BlockSpec((r.shape[0], SPAN), lambda i: (0, first(i))) for r in rows]
         + gate
         + down,
-        out_specs=[pl.BlockSpec((n, WIDE), lambda i: (0, second(i))) for n in parts],
+        out_specs=[pl.BlockSpec((n, SPAN), lambda i: (0, second(i))) for n in parts],
         scratch_shapes=scratch,
         compiler_params=VMEM,
         cost_estimate=LIGHT,

time: 265 us -> 261 us (0.985)
  Pallas kernels: 60.3 us -> 53 us
  waiting for transfers between devices: 116 us -> 120 us
    pallas_call x2, Pallas kernels: 38.1 us -> 30.7 us  [through_expert(): pl.pallas_call(functools.partial(kernel, steps), grid=(2 * steps,), out_s...]
    ppermute x23, waiting for transfers between devices: 96.4 us -> 99.9 us  [move(): return lax.ppermute(block, ('pp', 'ep'), route)]
  transfers between devices with their start and end apart: 26 -> 26, of which waited for: 12 -> 12; matrix products, arithmetic and copies ran while one was open for 1% -> 2% of each run, Pallas kernels for 22% -> 20%
where the time goes in v2:
time: 261 us; the launch traced here: 260 us
  waiting for transfers between devices  120 us (46%)
  starting transfers between devices  61.9 us (24%)
  Pallas kernels  53 us (20%)
  local copies, waits for them, and re-layouts  20.7 us (8%)
  other arithmetic  3.4 us (1%)
    ppermute x23, waiting for transfers between devices, move(): return lax.ppermute(block, ('pp', 'ep'), route)  99.9 us
    ppermute x23, starting transfers between devices, move(): return lax.ppermute(block, ('pp', 'ep'), route)  47.9 us
    pallas_call x2, Pallas kernels, through_expert(): pl.pallas_call(functools.partial(kernel, steps), grid=(2 * steps,), out_s...  30.7 us
    pallas_call x14, Pallas kernels, whole(): pl.pallas_call(kernel, out_shape=outs, in_specs=[pl.BlockSpec(memory_spac...  22.3 us
    unnamed x50, local copies, waits for them, and re-layouts  20.1 us
    all_to_all x3, waiting for transfers between devices, along_y(): lax.all_to_all(rows.reshape(shape), 'ep', 0, 0, axis_index_groups=groups,...  19.8 us
    all_to_all x3, starting transfers between devices, along_y(): lax.all_to_all(rows.reshape(shape), 'ep', 0, 0, axis_index_groups=groups,...  14 us
  transfers between devices with their start and end apart: 26, of which 12 were waited for; matrix products, arithmetic and copies ran while one was open for 2% of the time, Pallas kernels for 20%

profile of v2, /device:TPU:0, one launch (start us, length us, event | category | flops | bytes accessed | tf_op | source)
XLA Modules:
  0.0 259.6 jit_solution(2450658758321021386)
XLA Ops:
  0.6 3.2 %collective-permute-start.4 = (bf16[128,7168]{1,0:T(8,128)(2,1)}, bf16[128,7168]{1,0:T(8,128)(2,1)}, u32[]{:S(2)}, u32[]{:S(2)}) collective-permute-start(bf16[128,7168]{1,0:T(8,128)(2,1)} %bitcast.31), channel_id=1, source_target_pairs={{0,2},{1,3},{2,0},{3,1},{4,6},{5,7},{6,4},{7,5},{8,10},{9,11},{10,... | collective-permute-start | bytes 5505032 | tf_op jit(solution)/shard_map/ppermute | solution.py:31
  11.8 4.6 %all-to-all-start = ((bf16[4,32,7168]{2,1,0:T(8,128)(2,1)}), bf16[4,32,7168]{2,1,0:T(8,128)(2,1)}, u32[]{:S(2)}, u32[]{:S(2)}) async-start(bf16[4,32,7168]{2,1,0:T(8,128)(2,1)} %bitcast.7), calls=%async_computation | async-start | bytes 3670016 | tf_op jit(solution)/shard_map/all_to_all | solution.py:315
  22.4 21.8 %collective-permute-done.5.far_order = s32[1,128]{1,0:T(1,128)S(1)} collective-permute-done((s32[1,128]{1,0:T(1,128)S(1)}, s32[1,128]{1,0:T(1,128)S(1)}, u32[]{:S(2)}, u32[]{:S(2)}) %collective-permute-start.5) | collective-permute-done | bytes 544 | tf_op jit(solution)/shard_map/ppermute | solution.py:31
  44.2 4.7 %all-to-all-start.1 = ((bf16[4,32,7168]{2,1,0:T(8,128)(2,1)}), bf16[4,32,7168]{2,1,0:T(8,128)(2,1)}, u32[]{:S(2)}, u32[]{:S(2)}) async-start(bf16[4,32,7168]{2,1,0:T(8,128)(2,1)} %bitcast.33), calls=%async_computation.1 | async-start | bytes 3670016 | tf_op jit(solution)/shard_map/all_to_all | solution.py:315
  51.9 19.8 %all-to-all-done.1 = bf16[4,32,7168]{2,1,0:T(8,128)(2,1)} async-done(((bf16[4,32,7168]{2,1,0:T(8,128)(2,1)}), bf16[4,32,7168]{2,1,0:T(8,128)(2,1)}, u32[]{:S(2)}, u32[]{:S(2)}) %all-to-all-start.1) | async-done | bytes 1835040 | tf_op jit(solution)/shard_map/all_to_all | solution.py:315
  79.3 4.7 %all-to-all-start.2 = ((bf16[4,64,7168]{2,1,0:T(8,128)(2,1)}), bf16[4,64,7168]{2,1,0:T(8,128)(2,1)}, u32[]{:S(2)}, u32[]{:S(2)}) async-start(bf16[4,64,7168]{2,1,0:T(8,128)(2,1)} %bitcast.30), calls=%async_computation.2 | async-start | bytes 7340032 | tf_op jit(solution)/shard_map/all_to_all | solution.py:315
  84.1 7.3 %collective-permute-done.far = bf16[128,7168]{1,0:T(8,128)(2,1)} collective-permute-done((bf16[128,7168]{1,0:T(8,128)(2,1)}, bf16[128,7168]{1,0:T(8,128)(2,1)}, u32[]{:S(2)}, u32[]{:S(2)}) %collective-permute-start) | collective-permute-done | bytes 1835040 | tf_op jit(solution)/shard_map/ppermute | solution.py:31
  91.3 3.2 %collective-permute-start.6 = (bf16[128,7168]{1,0:T(8,128)(2,1)}, bf16[128,7168]{1,0:T(8,128)(2,1)S(1)}, u32[]{:S(2)}, u32[]{:S(2)}) collective-permute-start(bf16[128,7168]{1,0:T(8,128)(2,1)} %bitcast.17.near), channel_id=1, source_target_pairs={{0,2},{1,3},{2,0},{3,1},{4,6},{5,7},{6,4},{7,5},{8,10},{9,11},{10,... | collective-permute-start | bytes 5505032 | tf_op jit(solution)/shard_map/ppermute | solution.py:31
  96.6 12.9 %shard_map.132 = (bf16[64,7168]{1,0:T(8,128)(2,1)S(1)}, bf16[64,7168]{1,0:T(8,128)(2,1)S(1)}, bf16[64,7168]{1,0:T(8,128)(2,1)}, bf16[64,7168]{1,0:T(8,128)(2,1)}) custom-call(s32[1]{0:T(128)} %bitcast.6.place, bf16[128,7168]{1,0:T(8,128)(2,1)} %bitcast.8.near, bf16[128,7168]{1,0:T(8,128)(2,1)} %collective-permute-done.far, bf16[7168,256]{1,0:T(8,128)(2,1)S(1)} %bitcast.29, ...), custom_call_target="tpu_custom_call" | custom-call | flops 1000 | bytes 1000 | tf_op jit(solution)/shard_map/pallas_call | solution.py:275
  110.8 25.2 %collective-permute-done.6.far = bf16[128,7168]{1,0:T(8,128)(2,1)S(1)} collective-permute-done((bf16[128,7168]{1,0:T(8,128)(2,1)}, bf16[128,7168]{1,0:T(8,128)(2,1)S(1)}, u32[]{:S(2)}, u32[]{:S(2)}) %collective-permute-start.6) | collective-permute-done | bytes 1835040 | tf_op jit(solution)/shard_map/ppermute | solution.py:31
  138.8 17.8 %shard_map.135 = (bf16[64,7168]{1,0:T(8,128)(2,1)S(1)}, bf16[32,7168]{1,0:T(8,128)(2,1)S(1)}, bf16[32,7168]{1,0:T(8,128)(2,1)S(1)}, bf16[64,7168]{1,0:T(8,128)(2...) custom-call(s32[1]{0:T(128)} %bitcast.6.place, bf16[128,7168]{1,0:T(8,128)(2,1)} %bitcast.17.near, ...), custom_call_target="tpu_custom_call" | custom-call | flops 1000 | bytes 1000 | tf_op jit(solution)/shard_map/pallas_call | solution.py:275
  156.6 3.3 %collective-permute-start.9 = (bf16[64,7168]{1,0:T(8,128)(2,1)S(1)}, bf16[64,7168]{1,0:T(8,128)(2,1)S(1)}, u32[]{:S(2)}, u32[]{:S(2)}) collective-permute-start(bf16[64,7168]{1,0:T(8,128)(2,1)S(1)} %get-tuple-element.64), channel_id=1, source_target_pairs={{0,2},{1,3},{2,0},{3,1},{4,6},{5,7},{6,4},{7,5},{8,10},{9,11},{10,... | collective-permute-start | bytes 2752520 | tf_op jit(solution)/shard_map/ppermute | solution.py:31
  162.5 3.2 %collective-permute-start.8 = (bf16[32,7168]{1,0:T(8,128)(2,1)}, bf16[32,7168]{1,0:T(8,128)(2,1)}, u32[]{:S(2)}, u32[]{:S(2)}) collective-permute-start(bf16[32,7168]{1,0:T(8,128)(2,1)} %get-tuple-element.59), channel_id=1, source_target_pairs={{0,12},{1,13},{2,14},{3,15},{4,0},{5,1},{6,2},{7,3},{8,4},{9,5},{1... | collective-permute-start | bytes 1376264 | tf_op jit(solution)/shard_map/ppermute | solution.py:31
  165.7 13.8 %collective-permute-done.9.far = bf16[64,7168]{1,0:T(8,128)(2,1)S(1)} collective-permute-done((bf16[64,7168]{1,0:T(8,128)(2,1)S(1)}, bf16[64,7168]{1,0:T(8,128)(2,1)S(1)}, u32[]{:S(2)}, u32[]{:S(2)}) %collective-permute-start.9) | collective-permute-done | bytes 917536 | tf_op jit(solution)/shard_map/ppermute | solution.py:31
  186.8 3.2 %collective-permute-start.16 = (bf16[64,7168]{1,0:T(8,128)(2,1)}, bf16[64,7168]{1,0:T(8,128)(2,1)}, u32[]{:S(2)}, u32[]{:S(2)}) collective-permute-start(bf16[64,7168]{1,0:T(8,128)(2,1)} %get-tuple-element.77), channel_id=1, source_target_pairs={{0,2},{1,3},{2,0},{3,1},{4,6},{5,7},{6,4},{7,5},{8,10},{9,11},{10,... | collective-permute-start | bytes 2752520 | tf_op jit(solution)/shard_map/ppermute | solution.py:31
  199.0 4.1 %collective-permute-start.18 = (bf16[64,7296]{1,0:T(8,128)(2,1)S(1)}, bf16[64,7296]{1,0:T(8,128)(2,1)S(1)}, u32[]{:S(2)}, u32[]{:S(2)}) collective-permute-start(bf16[64,7296]{1,0:T(8,128)(2,1)S(1)} %shard_map.140), channel_id=1, source_target_pairs={{0,112},{1,113},{2,114},{3,115},{4,116},{5,117},{6,118},{7,119},{8... | collective-permute-start | bytes 2801672 | tf_op jit(solution)/shard_map/ppermute | solution.py:31
  203.2 3.2 %collective-permute-start.13 = (bf16[32,7168]{1,0:T(8,128)(2,1)S(1)}, bf16[32,7168]{1,0:T(8,128)(2,1)S(1)}, u32[]{:S(2)}, u32[]{:S(2)}) collective-permute-start(bf16[32,7168]{1,0:T(8,128)(2,1)S(1)} %shard_map.138), channel_id=1, source_target_pairs={{0,8},{1,9},{2,10},{3,11},{4,12},{5,13},{6,14},{7,15},{8,0},{9,1},... | collective-permute-start | bytes 1376264 | tf_op jit(solution)/shard_map/ppermute | solution.py:31
  208.4 8.5 %collective-permute-done.13.refs_0_ = bf16[32,7168]{1,0:T(8,128)(2,1)S(1)} collective-permute-done((bf16[32,7168]{1,0:T(8,128)(2,1)S(1)}, bf16[32,7168]{1,0:T(8,128)(2,1)S(1)}, u32[]{:S(2)}, u32[]{:S(2)}) %collective-permute-start.13) | collective-permute-done | bytes 458784 | tf_op jit(solution)/shard_map/ppermute | solution.py:31
  219.1 4.3 %collective-permute-start.17 = (bf16[32,7168]{1,0:T(8,128)(2,1)S(1)}, bf16[32,7168]{1,0:T(8,128)(2,1)S(1)}, u32[]{:S(2)}, u32[]{:S(2)}) collective-permute-start(bf16[32,7168]{1,0:T(8,128)(2,1)S(1)} %get-tuple-element.78), channel_id=1, source_target_pairs={{0,8},{1,9},{2,10},{3,11},{4,12},{5,13},{6,14},{7,15},{8,0},{9,1},... | collective-permute-start | bytes 1376264 | tf_op jit(solution)/shard_map/ppermute | solution.py:31
  223.4 4.8 %collective-permute-done.18.refs_0_ = bf16[64,7296]{1,0:T(8,128)(2,1)S(1)} collective-permute-done((bf16[64,7296]{1,0:T(8,128)(2,1)S(1)}, bf16[64,7296]{1,0:T(8,128)(2,1)S(1)}, u32[]{:S(2)}, u32[]{:S(2)}) %collective-permute-start.18) | collective-permute-done | bytes 933920 | tf_op jit(solution)/shard_map/ppermute | solution.py:31
  228.3 5.7 %collective-permute-done.19.refs_1_ = bf16[32,7168]{1,0:T(8,128)(2,1)S(1)} collective-permute-done((bf16[32,7168]{1,0:T(8,128)(2,1)S(1)}, bf16[32,7168]{1,0:T(8,128)(2,1)S(1)}, u32[]{:S(2)}, u32[]{:S(2)}) %collective-permute-start.19) | collective-permute-done | bytes 458784 | tf_op jit(solution)/shard_map/ppermute | solution.py:31
  235.2 8.6 %collective-permute-start.21 = (bf16[32,7296]{1,0:T(8,128)(2,1)S(1)}, bf16[32,7296]{1,0:T(8,128)(2,1)S(1)}, u32[]{:S(2)}, u32[]{:S(2)}) collective-permute-start(bf16[32,7296]{1,0:T(8,128)(2,1)S(1)} %shard_map.141), channel_id=1, source_target_pairs={{0,112},{1,113},{2,114},{3,115},{4,116},{5,117},{6,118},{7,119},{8... | collective-permute-start | bytes 1400840 | tf_op jit(solution)/shard_map/ppermute | solution.py:31
  245.7 4.1 %collective-permute-done.21.refs_1_ = bf16[32,7296]{1,0:T(8,128)(2,1)S(1)} collective-permute-done((bf16[32,7296]{1,0:T(8,128)(2,1)S(1)}, bf16[32,7296]{1,0:T(8,128)(2,1)S(1)}, u32[]{:S(2)}, u32[]{:S(2)}) %collective-permute-start.21) | collective-permute-done | bytes 466976 | tf_op jit(solution)/shard_map/ppermute | solution.py:31
  249.9 5.0 %collective-permute-done.22.refs_2_ = bf16[32,7296]{1,0:T(8,128)(2,1)S(1)} collective-permute-done((bf16[32,7296]{1,0:T(8,128)(2,1)S(1)}, bf16[32,7296]{1,0:T(8,128)(2,1)S(1)}, u32[]{:S(2)}, u32[]{:S(2)}) %collective-permute-start.22) | collective-permute-done | bytes 466976 | tf_op jit(solution)/shard_map/ppermute | solution.py:31
  (113 shorter events, 61.5 us)
Async XLA Ops:
  0.6 43.5 %collective-permute-start.4 = (bf16[128,7168]{1,0:T(8,128)(2,1)}, bf16[128,7168]{1,0:T(8,128)(2,1)}, u32[]{:S(2)}, u32[]{:S(2)}) collective-permute-start(bf16[128,7168]{1,0:T(8,128)(2,1)} %bitcast.31), channel_id=1, source_target_pairs={{0,2},{1,3},{2,0},{3,1},{4,6},{5,7},{6,4},{7,5},{8,10},{9,11},{10,... | collective-permute-start | bytes 5505032 | tf_op jit(solution)/shard_map/ppermute | solution.py:31
  11.8 32.3 %all-to-all-start = ((bf16[4,32,7168]{2,1,0:T(8,128)(2,1)}), bf16[4,32,7168]{2,1,0:T(8,128)(2,1)}, u32[]{:S(2)}, u32[]{:S(2)}) async-start(bf16[4,32,7168]{2,1,0:T(8,128)(2,1)} %bitcast.7), calls=%async_computation | async-start | bytes 3670016 | tf_op jit(solution)/shard_map/all_to_all | solution.py:315
  16.4 27.7 %collective-permute-start.5 = (s32[1,128]{1,0:T(1,128)S(1)}, s32[1,128]{1,0:T(1,128)S(1)}, u32[]{:S(2)}, u32[]{:S(2)}) collective-permute-start(s32[1,128]{1,0:T(1,128)S(1)} %multiply_add_fusion.expert_order.near_order), channel_id=1, source_target_pairs={{0,2},{1,3},{2,0},{3,1},{4,6},{5,7},{6,4},{7,5},{8,10},{9,11},{10,... | collective-permute-start | bytes 1544 | tf_op jit(solution)/shard_map/ppermute | solution.py:31
  17.0 77.6 %collective-permute-start.1 = (bf16[7168,256]{1,0:T(8,128)(2,1)}, bf16[7168,256]{1,0:T(8,128)(2,1)}, u32[]{:S(2)}, u32[]{:S(2)}) collective-permute-start(bf16[7168,256]{1,0:T(8,128)(2,1)} %bitcast.27), channel_id=1, source_target_pairs={{0,1},{1,0},{2,3},{3,2},{4,5},{5,4},{6,7},{7,6},{8,9},{9,8},{10,11... | collective-permute-start | bytes 11010056 | tf_op jit(solution)/shard_map/ppermute | solution.py:31
  17.0 77.6 %collective-permute-start.2 = (bf16[7168,256]{1,0:T(8,128)(2,1)}, bf16[7168,256]{1,0:T(8,128)(2,1)}, u32[]{:S(2)}, u32[]{:S(2)}) collective-permute-start(bf16[7168,256]{1,0:T(8,128)(2,1)} %bitcast.39), channel_id=1, source_target_pairs={{0,1},{1,0},{2,3},{3,2},{4,5},{5,4},{6,7},{7,6},{8,9},{9,8},{10,11... | collective-permute-start | bytes 11010056 | tf_op jit(solution)/shard_map/ppermute | solution.py:31
  17.5 77.0 %collective-permute-start.3 = (bf16[256,7168]{1,0:T(8,128)(2,1)}, bf16[256,7168]{1,0:T(8,128)(2,1)}, u32[]{:S(2)}, u32[]{:S(2)}) collective-permute-start(bf16[256,7168]{1,0:T(8,128)(2,1)} %bitcast.42), channel_id=1, source_target_pairs={{0,1},{1,0},{2,3},{3,2},{4,5},{5,4},{6,7},{7,6},{8,9},{9,8},{10,11... | collective-permute-start | bytes 11010056 | tf_op jit(solution)/shard_map/ppermute | solution.py:31
  44.2 27.5 %all-to-all-start.1 = ((bf16[4,32,7168]{2,1,0:T(8,128)(2,1)}), bf16[4,32,7168]{2,1,0:T(8,128)(2,1)}, u32[]{:S(2)}, u32[]{:S(2)}) async-start(bf16[4,32,7168]{2,1,0:T(8,128)(2,1)} %bitcast.33), calls=%async_computation.1 | async-start | bytes 3670016 | tf_op jit(solution)/shard_map/all_to_all | solution.py:315
  48.8 42.5 %collective-permute-start = (bf16[128,7168]{1,0:T(8,128)(2,1)}, bf16[128,7168]{1,0:T(8,128)(2,1)}, u32[]{:S(2)}, u32[]{:S(2)}) collective-permute-start(bf16[128,7168]{1,0:T(8,128)(2,1)} %bitcast.8.near), channel_id=1, source_target_pairs={{0,2},{1,3},{2,0},{3,1},{4,6},{5,7},{6,4},{7,5},{8,10},{9,11},{10,... | collective-permute-start | bytes 5505032 | tf_op jit(solution)/shard_map/ppermute | solution.py:31
  79.3 58.0 %all-to-all-start.2 = ((bf16[4,64,7168]{2,1,0:T(8,128)(2,1)}), bf16[4,64,7168]{2,1,0:T(8,128)(2,1)}, u32[]{:S(2)}, u32[]{:S(2)}) async-start(bf16[4,64,7168]{2,1,0:T(8,128)(2,1)} %bitcast.30), calls=%async_computation.2 | async-start | bytes 7340032 | tf_op jit(solution)/shard_map/all_to_all | solution.py:315
  91.3 44.7 %collective-permute-start.6 = (bf16[128,7168]{1,0:T(8,128)(2,1)}, bf16[128,7168]{1,0:T(8,128)(2,1)S(1)}, u32[]{:S(2)}, u32[]{:S(2)}) collective-permute-start(bf16[128,7168]{1,0:T(8,128)(2,1)} %bitcast.17.near), channel_id=1, source_target_pairs={{0,2},{1,3},{2,0},{3,1},{4,6},{5,7},{6,4},{7,5},{8,10},{9,11},{10,... | collective-permute-start | bytes 5505032 | tf_op jit(solution)/shard_map/ppermute | solution.py:31
  110.5 46.1 %collective-permute-start.7 = (bf16[64,7168]{1,0:T(8,128)(2,1)}, bf16[64,7168]{1,0:T(8,128)(2,1)}, u32[]{:S(2)}, u32[]{:S(2)}) collective-permute-start(bf16[64,7168]{1,0:T(8,128)(2,1)} %get-tuple-element.58), channel_id=1, source_target_pairs={{0,2},{1,3},{2,0},{3,1},{4,6},{5,7},{6,4},{7,5},{8,10},{9,11},{10,... | collective-permute-start | bytes 2752520 | tf_op jit(solution)/shard_map/ppermute | solution.py:31
  156.6 22.9 %collective-permute-start.9 = (bf16[64,7168]{1,0:T(8,128)(2,1)S(1)}, bf16[64,7168]{1,0:T(8,128)(2,1)S(1)}, u32[]{:S(2)}, u32[]{:S(2)}) collective-permute-start(bf16[64,7168]{1,0:T(8,128)(2,1)S(1)} %get-tuple-element.64), channel_id=1, source_target_pairs={{0,2},{1,3},{2,0},{3,1},{4,6},{5,7},{6,4},{7,5},{8,10},{9,11},{10,... | collective-permute-start | bytes 2752520 | tf_op jit(solution)/shard_map/ppermute | solution.py:31
  159.9 26.1 %collective-permute-start.10 = (bf16[32,7168]{1,0:T(8,128)(2,1)S(1)}, bf16[32,7168]{1,0:T(8,128)(2,1)S(1)}, u32[]{:S(2)}, u32[]{:S(2)}) collective-permute-start(bf16[32,7168]{1,0:T(8,128)(2,1)S(1)} %get-tuple-element.67), channel_id=1, source_target_pairs={{0,2},{1,3},{2,0},{3,1},{4,6},{5,7},{6,4},{7,5},{8,10},{9,11},{10,... | collective-permute-start | bytes 1376264 | tf_op jit(solution)/shard_map/ppermute | solution.py:31
  162.5 30.5 %collective-permute-start.8 = (bf16[32,7168]{1,0:T(8,128)(2,1)}, bf16[32,7168]{1,0:T(8,128)(2,1)}, u32[]{:S(2)}, u32[]{:S(2)}) collective-permute-start(bf16[32,7168]{1,0:T(8,128)(2,1)} %get-tuple-element.59), channel_id=1, source_target_pairs={{0,12},{1,13},{2,14},{3,15},{4,0},{5,1},{6,2},{7,3},{8,4},{9,5},{1... | collective-permute-start | bytes 1376264 | tf_op jit(solution)/shard_map/ppermute | solution.py:31
  165.7 27.2 %collective-permute-start.11 = (bf16[32,7168]{1,0:T(8,128)(2,1)}, bf16[32,7168]{1,0:T(8,128)(2,1)}, u32[]{:S(2)}, u32[]{:S(2)}) collective-permute-start(bf16[32,7168]{1,0:T(8,128)(2,1)} %get-tuple-element.61), channel_id=1, source_target_pairs={{0,4},{1,5},{2,6},{3,7},{4,8},{5,9},{6,10},{7,11},{8,12},{9,13},{1... | collective-permute-start | bytes 1376264 | tf_op jit(solution)/shard_map/ppermute | solution.py:31
  180.6 15.5 %collective-permute-start.14 = (bf16[32,7168]{1,0:T(8,128)(2,1)}, bf16[32,7168]{1,0:T(8,128)(2,1)}, u32[]{:S(2)}, u32[]{:S(2)}) collective-permute-start(bf16[32,7168]{1,0:T(8,128)(2,1)} %get-tuple-element.72), channel_id=1, source_target_pairs={{0,12},{1,13},{2,14},{3,15},{4,0},{5,1},{6,2},{7,3},{8,4},{9,5},{1... | collective-permute-start | bytes 1376264 | tf_op jit(solution)/shard_map/ppermute | solution.py:31
  186.8 30.9 %collective-permute-start.16 = (bf16[64,7168]{1,0:T(8,128)(2,1)}, bf16[64,7168]{1,0:T(8,128)(2,1)}, u32[]{:S(2)}, u32[]{:S(2)}) collective-permute-start(bf16[64,7168]{1,0:T(8,128)(2,1)} %get-tuple-element.77), channel_id=1, source_target_pairs={{0,2},{1,3},{2,0},{3,1},{4,6},{5,7},{6,4},{7,5},{8,10},{9,11},{10,... | collective-permute-start | bytes 2752520 | tf_op jit(solution)/shard_map/ppermute | solution.py:31
  199.0 29.2 %collective-permute-start.18 = (bf16[64,7296]{1,0:T(8,128)(2,1)S(1)}, bf16[64,7296]{1,0:T(8,128)(2,1)S(1)}, u32[]{:S(2)}, u32[]{:S(2)}) collective-permute-start(bf16[64,7296]{1,0:T(8,128)(2,1)S(1)} %shard_map.140), channel_id=1, source_target_pairs={{0,112},{1,113},{2,114},{3,115},{4,116},{5,117},{6,118},{7,119},{8... | collective-permute-start | bytes 2801672 | tf_op jit(solution)/shard_map/ppermute | solution.py:31
  203.2 31.5 %collective-permute-start.12 = (bf16[64,7296]{1,0:T(8,128)(2,1)S(1)}, bf16[64,7296]{1,0:T(8,128)(2,1)S(1)}, u32[]{:S(2)}, u32[]{:S(2)}) collective-permute-start(bf16[64,7296]{1,0:T(8,128)(2,1)S(1)} %shard_map.139), channel_id=1, source_target_pairs={{0,16},{1,17},{2,18},{3,19},{4,20},{5,21},{6,22},{7,23},{8,24},{9,... | collective-permute-start | bytes 2801672 | tf_op jit(solution)/shard_map/ppermute | solution.py:31
  203.2 13.7 %collective-permute-start.13 = (bf16[32,7168]{1,0:T(8,128)(2,1)S(1)}, bf16[32,7168]{1,0:T(8,128)(2,1)S(1)}, u32[]{:S(2)}, u32[]{:S(2)}) collective-permute-start(bf16[32,7168]{1,0:T(8,128)(2,1)S(1)} %shard_map.138), channel_id=1, source_target_pairs={{0,8},{1,9},{2,10},{3,11},{4,12},{5,13},{6,14},{7,15},{8,0},{9,1},... | collective-permute-start | bytes 1376264 | tf_op jit(solution)/shard_map/ppermute | solution.py:31
  206.4 27.6 %collective-permute-start.19 = (bf16[32,7168]{1,0:T(8,128)(2,1)S(1)}, bf16[32,7168]{1,0:T(8,128)(2,1)S(1)}, u32[]{:S(2)}, u32[]{:S(2)}) collective-permute-start(bf16[32,7168]{1,0:T(8,128)(2,1)S(1)} %copy-done.20), channel_id=1, source_target_pairs={{0,2},{1,3},{2,0},{3,1},{4,6},{5,7},{6,4},{7,5},{8,10},{9,11},{10,... | collective-permute-start | bytes 1376264 | tf_op jit(solution)/shard_map/ppermute | solution.py:31
  219.1 15.6 %collective-permute-start.17 = (bf16[32,7168]{1,0:T(8,128)(2,1)S(1)}, bf16[32,7168]{1,0:T(8,128)(2,1)S(1)}, u32[]{:S(2)}, u32[]{:S(2)}) collective-permute-start(bf16[32,7168]{1,0:T(8,128)(2,1)S(1)} %get-tuple-element.78), channel_id=1, source_target_pairs={{0,8},{1,9},{2,10},{3,11},{4,12},{5,13},{6,14},{7,15},{8,0},{9,1},... | collective-permute-start | bytes 1376264 | tf_op jit(solution)/shard_map/ppermute | solution.py:31
  235.1 22.6 %collective-permute-start.20 = (bf16[64,7296]{1,0:T(8,128)(2,1)S(1)}, bf16[64,7296]{1,0:T(8,128)(2,1)S(1)}, u32[]{:S(2)}, u32[]{:S(2)}) collective-permute-start(bf16[64,7296]{1,0:T(8,128)(2,1)S(1)} %shard_map.144), channel_id=1, source_target_pairs={{0,16},{1,17},{2,18},{3,19},{4,20},{5,21},{6,22},{7,23},{8,24},{9,... | collective-permute-start | bytes 2801672 | tf_op jit(solution)/shard_map/ppermute | solution.py:31
  235.2 14.7 %collective-permute-start.21 = (bf16[32,7296]{1,0:T(8,128)(2,1)S(1)}, bf16[32,7296]{1,0:T(8,128)(2,1)S(1)}, u32[]{:S(2)}, u32[]{:S(2)}) collective-permute-start(bf16[32,7296]{1,0:T(8,128)(2,1)S(1)} %shard_map.141), channel_id=1, source_target_pairs={{0,112},{1,113},{2,114},{3,115},{4,116},{5,117},{6,118},{7,119},{8... | collective-permute-start | bytes 1400840 | tf_op jit(solution)/shard_map/ppermute | solution.py:31
  (27 other events, 200.9 us)

commit v3 on v2

--- a/solution.py
+++ b/solution.py
@@ -350,7 +350,7 @@
         far_order,
         back_turn,
     )
-    back_far = cross(back_near, pairs, ahead_far)
+    back_far = cross(back_near)
     pairs = along_y(pairs)
 
     ahead_groups, back_groups = (2 * cap, 2 * cap), (2 * cap, cap, cap)

time: 261 us -> 259 us (level)
  waiting for transfers between devices: 120 us -> 117 us
    ppermute x23, waiting for transfers between devices: 99.9 us -> 96.8 us  [move(): return lax.ppermute(block, ('pp', 'ep'), route)]
where the time goes in v3:
time: 259 us; the launch traced here: 258 us
  waiting for transfers between devices  117 us (45%)
  starting transfers between devices  63.6 us (25%)
  Pallas kernels  53 us (20%)
  local copies, waits for them, and re-layouts  20.7 us (8%)
  other arithmetic  3.4 us (1%)
    ppermute x23, waiting for transfers between devices, move(): return lax.ppermute(block, ('pp', 'ep'), route)  96.8 us
    ppermute x23, starting transfers between devices, move(): return lax.ppermute(block, ('pp', 'ep'), route)  49.5 us
    pallas_call x2, Pallas kernels, through_expert(): pl.pallas_call(functools.partial(kernel, steps), grid=(2 * steps,), out_s...  30.7 us
    pallas_call x14, Pallas kernels, whole(): pl.pallas_call(kernel, out_shape=outs, in_specs=[pl.BlockSpec(memory_spac...  22.3 us
    unnamed x50, local copies, waits for them, and re-layouts  20.1 us
    all_to_all x3, waiting for transfers between devices, along_y(): lax.all_to_all(rows.reshape(shape), 'ep', 0, 0, axis_index_groups=groups,...  19.8 us
    all_to_all x3, starting transfers between devices, along_y(): lax.all_to_all(rows.reshape(shape), 'ep', 0, 0, axis_index_groups=groups,...  14 us
  transfers between devices with their start and end apart: 26, of which 12 were waited for; matrix products, arithmetic and copies ran while one was open for 2% of the time, Pallas kernels for 20%

profile of v3, /device:TPU:0, one launch (start us, length us, event | category | flops | bytes accessed | tf_op | source)
XLA Modules:
  0.0 258.2 jit_solution(8978253064488016627)
XLA Ops:
  0.6 3.2 %collective-permute-start.4 = (bf16[128,7168]{1,0:T(8,128)(2,1)}, bf16[128,7168]{1,0:T(8,128)(2,1)}, u32[]{:S(2)}, u32[]{:S(2)}) collective-permute-start(bf16[128,7168]{1,0:T(8,128)(2,1)} %bitcast.31), channel_id=1, source_target_pairs={{0,2},{1,3},{2,0},{3,1},{4,6},{5,7},{6,4},{7,5},{8,10},{9,11},{10,... | collective-permute-start | bytes 5505032 | tf_op jit(solution)/shard_map/ppermute | solution.py:31
  11.8 4.6 %all-to-all-start = ((bf16[4,32,7168]{2,1,0:T(8,128)(2,1)}), bf16[4,32,7168]{2,1,0:T(8,128)(2,1)}, u32[]{:S(2)}, u32[]{:S(2)}) async-start(bf16[4,32,7168]{2,1,0:T(8,128)(2,1)} %bitcast.7), calls=%async_computation | async-start | bytes 3670016 | tf_op jit(solution)/shard_map/all_to_all | solution.py:315
  22.4 21.7 %collective-permute-done.5.far_order = s32[1,128]{1,0:T(1,128)S(1)} collective-permute-done((s32[1,128]{1,0:T(1,128)S(1)}, s32[1,128]{1,0:T(1,128)S(1)}, u32[]{:S(2)}, u32[]{:S(2)}) %collective-permute-start.5) | collective-permute-done | bytes 544 | tf_op jit(solution)/shard_map/ppermute | solution.py:31
  44.2 4.7 %all-to-all-start.1 = ((bf16[4,32,7168]{2,1,0:T(8,128)(2,1)}), bf16[4,32,7168]{2,1,0:T(8,128)(2,1)}, u32[]{:S(2)}, u32[]{:S(2)}) async-start(bf16[4,32,7168]{2,1,0:T(8,128)(2,1)} %bitcast.33), calls=%async_computation.1 | async-start | bytes 3670016 | tf_op jit(solution)/shard_map/all_to_all | solution.py:315
  51.9 19.8 %all-to-all-done.1 = bf16[4,32,7168]{2,1,0:T(8,128)(2,1)} async-done(((bf16[4,32,7168]{2,1,0:T(8,128)(2,1)}), bf16[4,32,7168]{2,1,0:T(8,128)(2,1)}, u32[]{:S(2)}, u32[]{:S(2)}) %all-to-all-start.1) | async-done | bytes 1835040 | tf_op jit(solution)/shard_map/all_to_all | solution.py:315
  79.3 4.7 %all-to-all-start.2 = ((bf16[4,64,7168]{2,1,0:T(8,128)(2,1)}), bf16[4,64,7168]{2,1,0:T(8,128)(2,1)}, u32[]{:S(2)}, u32[]{:S(2)}) async-start(bf16[4,64,7168]{2,1,0:T(8,128)(2,1)} %bitcast.30), calls=%async_computation.2 | async-start | bytes 7340032 | tf_op jit(solution)/shard_map/all_to_all | solution.py:315
  84.1 3.2 %collective-permute-start.6 = (bf16[128,7168]{1,0:T(8,128)(2,1)}, bf16[128,7168]{1,0:T(8,128)(2,1)S(1)}, u32[]{:S(2)}, u32[]{:S(2)}) collective-permute-start(bf16[128,7168]{1,0:T(8,128)(2,1)} %bitcast.17.near), channel_id=1, source_target_pairs={{0,2},{1,3},{2,0},{3,1},{4,6},{5,7},{6,4},{7,5},{8,10},{9,11},{10,... | collective-permute-start | bytes 5505032 | tf_op jit(solution)/shard_map/ppermute | solution.py:31
  87.2 6.4 %collective-permute-done.far = bf16[128,7168]{1,0:T(8,128)(2,1)} collective-permute-done((bf16[128,7168]{1,0:T(8,128)(2,1)}, bf16[128,7168]{1,0:T(8,128)(2,1)}, u32[]{:S(2)}, u32[]{:S(2)}) %collective-permute-start) | collective-permute-done | bytes 1835040 | tf_op jit(solution)/shard_map/ppermute | solution.py:31
  95.7 12.9 %shard_map.132 = (bf16[64,7168]{1,0:T(8,128)(2,1)S(1)}, bf16[64,7168]{1,0:T(8,128)(2,1)S(1)}, bf16[64,7168]{1,0:T(8,128)(2,1)}, bf16[64,7168]{1,0:T(8,128)(2,1)}) custom-call(s32[1]{0:T(128)} %bitcast.6.place, bf16[128,7168]{1,0:T(8,128)(2,1)} %bitcast.8.near, bf16[128,7168]{1,0:T(8,128)(2,1)} %collective-permute-done.far, bf16[7168,256]{1,0:T(8,128)(2,1)S(1)} %bitcast.29, ...), custom_call_target="tpu_custom_call" | custom-call | flops 1000 | bytes 1000 | tf_op jit(solution)/shard_map/pallas_call | solution.py:275
  112.6 20.3 %collective-permute-done.6.far = bf16[128,7168]{1,0:T(8,128)(2,1)S(1)} collective-permute-done((bf16[128,7168]{1,0:T(8,128)(2,1)}, bf16[128,7168]{1,0:T(8,128)(2,1)S(1)}, u32[]{:S(2)}, u32[]{:S(2)}) %collective-permute-start.6) | collective-permute-done | bytes 1835040 | tf_op jit(solution)/shard_map/ppermute | solution.py:31
  135.6 17.8 %shard_map.135 = (bf16[64,7168]{1,0:T(8,128)(2,1)S(1)}, bf16[32,7168]{1,0:T(8,128)(2,1)S(1)}, bf16[32,7168]{1,0:T(8,128)(2,1)S(1)}, bf16[64,7168]{1,0:T(8,128)(2...) custom-call(s32[1]{0:T(128)} %bitcast.6.place, bf16[128,7168]{1,0:T(8,128)(2,1)} %bitcast.17.near, ...), custom_call_target="tpu_custom_call" | custom-call | flops 1000 | bytes 1000 | tf_op jit(solution)/shard_map/pallas_call | solution.py:275
  153.4 3.1 %collective-permute-start.9 = (bf16[64,7168]{1,0:T(8,128)(2,1)S(1)}, bf16[64,7168]{1,0:T(8,128)(2,1)S(1)}, u32[]{:S(2)}, u32[]{:S(2)}) collective-permute-start(bf16[64,7168]{1,0:T(8,128)(2,1)S(1)} %get-tuple-element.62), channel_id=1, source_target_pairs={{0,2},{1,3},{2,0},{3,1},{4,6},{5,7},{6,4},{7,5},{8,10},{9,11},{10,... | collective-permute-start | bytes 2752520 | tf_op jit(solution)/shard_map/ppermute | solution.py:31
  159.3 3.2 %collective-permute-start.8 = (bf16[32,7168]{1,0:T(8,128)(2,1)}, bf16[32,7168]{1,0:T(8,128)(2,1)}, u32[]{:S(2)}, u32[]{:S(2)}) collective-permute-start(bf16[32,7168]{1,0:T(8,128)(2,1)} %get-tuple-element.57), channel_id=1, source_target_pairs={{0,12},{1,13},{2,14},{3,15},{4,0},{5,1},{6,2},{7,3},{8,4},{9,5},{1... | collective-permute-start | bytes 1376264 | tf_op jit(solution)/shard_map/ppermute | solution.py:31
  162.5 15.4 %collective-permute-done.9.far = bf16[64,7168]{1,0:T(8,128)(2,1)S(1)} collective-permute-done((bf16[64,7168]{1,0:T(8,128)(2,1)S(1)}, bf16[64,7168]{1,0:T(8,128)(2,1)S(1)}, u32[]{:S(2)}, u32[]{:S(2)}) %collective-permute-start.9) | collective-permute-done | bytes 917536 | tf_op jit(solution)/shard_map/ppermute | solution.py:31
  183.7 3.2 %collective-permute-start.16 = (bf16[64,7168]{1,0:T(8,128)(2,1)}, bf16[64,7168]{1,0:T(8,128)(2,1)}, u32[]{:S(2)}, u32[]{:S(2)}) collective-permute-start(bf16[64,7168]{1,0:T(8,128)(2,1)} %get-tuple-element.75), channel_id=1, source_target_pairs={{0,2},{1,3},{2,0},{3,1},{4,6},{5,7},{6,4},{7,5},{8,10},{9,11},{10,... | collective-permute-start | bytes 2752520 | tf_op jit(solution)/shard_map/ppermute | solution.py:31
  195.9 4.1 %collective-permute-start.18 = (bf16[64,7296]{1,0:T(8,128)(2,1)S(1)}, bf16[64,7296]{1,0:T(8,128)(2,1)S(1)}, u32[]{:S(2)}, u32[]{:S(2)}) collective-permute-start(bf16[64,7296]{1,0:T(8,128)(2,1)S(1)} %shard_map.140), channel_id=1, source_target_pairs={{0,112},{1,113},{2,114},{3,115},{4,116},{5,117},{6,118},{7,119},{8... | collective-permute-start | bytes 2801672 | tf_op jit(solution)/shard_map/ppermute | solution.py:31
  200.0 3.3 %collective-permute-start.13 = (bf16[32,7168]{1,0:T(8,128)(2,1)S(1)}, bf16[32,7168]{1,0:T(8,128)(2,1)S(1)}, u32[]{:S(2)}, u32[]{:S(2)}) collective-permute-start(bf16[32,7168]{1,0:T(8,128)(2,1)S(1)} %shard_map.138), channel_id=1, source_target_pairs={{0,8},{1,9},{2,10},{3,11},{4,12},{5,13},{6,14},{7,15},{8,0},{9,1},... | collective-permute-start | bytes 1376264 | tf_op jit(solution)/shard_map/ppermute | solution.py:31
  205.3 4.7 %collective-permute-done.13.refs_0_ = bf16[32,7168]{1,0:T(8,128)(2,1)S(1)} collective-permute-done((bf16[32,7168]{1,0:T(8,128)(2,1)S(1)}, bf16[32,7168]{1,0:T(8,128)(2,1)S(1)}, u32[]{:S(2)}, u32[]{:S(2)}) %collective-permute-start.13) | collective-permute-done | bytes 458784 | tf_op jit(solution)/shard_map/ppermute | solution.py:31
  212.3 4.3 %collective-permute-start.17 = (bf16[32,7168]{1,0:T(8,128)(2,1)S(1)}, bf16[32,7168]{1,0:T(8,128)(2,1)S(1)}, u32[]{:S(2)}, u32[]{:S(2)}) collective-permute-start(bf16[32,7168]{1,0:T(8,128)(2,1)S(1)} %get-tuple-element.76), channel_id=1, source_target_pairs={{0,8},{1,9},{2,10},{3,11},{4,12},{5,13},{6,14},{7,15},{8,0},{9,1},... | collective-permute-start | bytes 1376264 | tf_op jit(solution)/shard_map/ppermute | solution.py:31
  216.6 10.3 %collective-permute-done.18.refs_0_ = bf16[64,7296]{1,0:T(8,128)(2,1)S(1)} collective-permute-done((bf16[64,7296]{1,0:T(8,128)(2,1)S(1)}, bf16[64,7296]{1,0:T(8,128)(2,1)S(1)}, u32[]{:S(2)}, u32[]{:S(2)}) %collective-permute-start.18) | collective-permute-done | bytes 933920 | tf_op jit(solution)/shard_map/ppermute | solution.py:31
  226.9 5.7 %collective-permute-done.19.refs_1_ = bf16[32,7168]{1,0:T(8,128)(2,1)S(1)} collective-permute-done((bf16[32,7168]{1,0:T(8,128)(2,1)S(1)}, bf16[32,7168]{1,0:T(8,128)(2,1)S(1)}, u32[]{:S(2)}, u32[]{:S(2)}) %collective-permute-start.19) | collective-permute-done | bytes 458784 | tf_op jit(solution)/shard_map/ppermute | solution.py:31
  233.8 7.1 %collective-permute-start.21 = (bf16[32,7296]{1,0:T(8,128)(2,1)S(1)}, bf16[32,7296]{1,0:T(8,128)(2,1)S(1)}, u32[]{:S(2)}, u32[]{:S(2)}) collective-permute-start(bf16[32,7296]{1,0:T(8,128)(2,1)S(1)} %shard_map.141), channel_id=1, source_target_pairs={{0,112},{1,113},{2,114},{3,115},{4,116},{5,117},{6,118},{7,119},{8... | collective-permute-start | bytes 1400840 | tf_op jit(solution)/shard_map/ppermute | solution.py:31
  242.8 5.2 %collective-permute-done.21.refs_1_ = bf16[32,7296]{1,0:T(8,128)(2,1)S(1)} collective-permute-done((bf16[32,7296]{1,0:T(8,128)(2,1)S(1)}, bf16[32,7296]{1,0:T(8,128)(2,1)S(1)}, u32[]{:S(2)}, u32[]{:S(2)}) %collective-permute-start.21) | collective-permute-done | bytes 466976 | tf_op jit(solution)/shard_map/ppermute | solution.py:31
  248.0 5.0 %collective-permute-done.22.refs_2_ = bf16[32,7296]{1,0:T(8,128)(2,1)S(1)} collective-permute-done((bf16[32,7296]{1,0:T(8,128)(2,1)S(1)}, bf16[32,7296]{1,0:T(8,128)(2,1)S(1)}, u32[]{:S(2)}, u32[]{:S(2)}) %collective-permute-start.22) | collective-permute-done | bytes 466976 | tf_op jit(solution)/shard_map/ppermute | solution.py:31
  (113 shorter events, 63.3 us)
Async XLA Ops:
  0.6 43.5 %collective-permute-start.4 = (bf16[128,7168]{1,0:T(8,128)(2,1)}, bf16[128,7168]{1,0:T(8,128)(2,1)}, u32[]{:S(2)}, u32[]{:S(2)}) collective-permute-start(bf16[128,7168]{1,0:T(8,128)(2,1)} %bitcast.31), channel_id=1, source_target_pairs={{0,2},{1,3},{2,0},{3,1},{4,6},{5,7},{6,4},{7,5},{8,10},{9,11},{10,... | collective-permute-start | bytes 5505032 | tf_op jit(solution)/shard_map/ppermute | solution.py:31
  11.8 32.3 %all-to-all-start = ((bf16[4,32,7168]{2,1,0:T(8,128)(2,1)}), bf16[4,32,7168]{2,1,0:T(8,128)(2,1)}, u32[]{:S(2)}, u32[]{:S(2)}) async-start(bf16[4,32,7168]{2,1,0:T(8,128)(2,1)} %bitcast.7), calls=%async_computation | async-start | bytes 3670016 | tf_op jit(solution)/shard_map/all_to_all | solution.py:315
  16.4 77.2 %collective-permute-start.1 = (bf16[7168,256]{1,0:T(8,128)(2,1)}, bf16[7168,256]{1,0:T(8,128)(2,1)}, u32[]{:S(2)}, u32[]{:S(2)}) collective-permute-start(bf16[7168,256]{1,0:T(8,128)(2,1)} %bitcast.27), channel_id=1, source_target_pairs={{0,1},{1,0},{2,3},{3,2},{4,5},{5,4},{6,7},{7,6},{8,9},{9,8},{10,11... | collective-permute-start | bytes 11010056 | tf_op jit(solution)/shard_map/ppermute | solution.py:31
  16.5 77.2 %collective-permute-start.2 = (bf16[7168,256]{1,0:T(8,128)(2,1)}, bf16[7168,256]{1,0:T(8,128)(2,1)}, u32[]{:S(2)}, u32[]{:S(2)}) collective-permute-start(bf16[7168,256]{1,0:T(8,128)(2,1)} %bitcast.39), channel_id=1, source_target_pairs={{0,1},{1,0},{2,3},{3,2},{4,5},{5,4},{6,7},{7,6},{8,9},{9,8},{10,11... | collective-permute-start | bytes 11010056 | tf_op jit(solution)/shard_map/ppermute | solution.py:31
  17.0 76.7 %collective-permute-start.3 = (bf16[256,7168]{1,0:T(8,128)(2,1)}, bf16[256,7168]{1,0:T(8,128)(2,1)}, u32[]{:S(2)}, u32[]{:S(2)}) collective-permute-start(bf16[256,7168]{1,0:T(8,128)(2,1)} %bitcast.42), channel_id=1, source_target_pairs={{0,1},{1,0},{2,3},{3,2},{4,5},{5,4},{6,7},{7,6},{8,9},{9,8},{10,11... | collective-permute-start | bytes 11010056 | tf_op jit(solution)/shard_map/ppermute | solution.py:31
  17.1 27.1 %collective-permute-start.5 = (s32[1,128]{1,0:T(1,128)S(1)}, s32[1,128]{1,0:T(1,128)S(1)}, u32[]{:S(2)}, u32[]{:S(2)}) collective-permute-start(s32[1,128]{1,0:T(1,128)S(1)} %multiply_add_fusion.expert_order.near_order), channel_id=1, source_target_pairs={{0,2},{1,3},{2,0},{3,1},{4,6},{5,7},{6,4},{7,5},{8,10},{9,11},{10,... | collective-permute-start | bytes 1544 | tf_op jit(solution)/shard_map/ppermute | solution.py:31
  44.2 27.5 %all-to-all-start.1 = ((bf16[4,32,7168]{2,1,0:T(8,128)(2,1)}), bf16[4,32,7168]{2,1,0:T(8,128)(2,1)}, u32[]{:S(2)}, u32[]{:S(2)}) async-start(bf16[4,32,7168]{2,1,0:T(8,128)(2,1)} %bitcast.33), calls=%async_computation.1 | async-start | bytes 3670016 | tf_op jit(solution)/shard_map/all_to_all | solution.py:315
  48.8 44.8 %collective-permute-start = (bf16[128,7168]{1,0:T(8,128)(2,1)}, bf16[128,7168]{1,0:T(8,128)(2,1)}, u32[]{:S(2)}, u32[]{:S(2)}) collective-permute-start(bf16[128,7168]{1,0:T(8,128)(2,1)} %bitcast.8.near), channel_id=1, source_target_pairs={{0,2},{1,3},{2,0},{3,1},{4,6},{5,7},{6,4},{7,5},{8,10},{9,11},{10,... | collective-permute-start | bytes 5505032 | tf_op jit(solution)/shard_map/ppermute | solution.py:31
  79.3 54.8 %all-to-all-start.2 = ((bf16[4,64,7168]{2,1,0:T(8,128)(2,1)}), bf16[4,64,7168]{2,1,0:T(8,128)(2,1)}, u32[]{:S(2)}, u32[]{:S(2)}) async-start(bf16[4,64,7168]{2,1,0:T(8,128)(2,1)} %bitcast.30), calls=%async_computation.2 | async-start | bytes 7340032 | tf_op jit(solution)/shard_map/all_to_all | solution.py:315
  84.1 48.8 %collective-permute-start.6 = (bf16[128,7168]{1,0:T(8,128)(2,1)}, bf16[128,7168]{1,0:T(8,128)(2,1)S(1)}, u32[]{:S(2)}, u32[]{:S(2)}) collective-permute-start(bf16[128,7168]{1,0:T(8,128)(2,1)} %bitcast.17.near), channel_id=1, source_target_pairs={{0,2},{1,3},{2,0},{3,1},{4,6},{5,7},{6,4},{7,5},{8,10},{9,11},{10,... | collective-permute-start | bytes 5505032 | tf_op jit(solution)/shard_map/ppermute | solution.py:31
  109.5 43.9 %collective-permute-start.7 = (bf16[64,7168]{1,0:T(8,128)(2,1)}, bf16[64,7168]{1,0:T(8,128)(2,1)}, u32[]{:S(2)}, u32[]{:S(2)}) collective-permute-start(bf16[64,7168]{1,0:T(8,128)(2,1)} %get-tuple-element.56), channel_id=1, source_target_pairs={{0,2},{1,3},{2,0},{3,1},{4,6},{5,7},{6,4},{7,5},{8,10},{9,11},{10,... | collective-permute-start | bytes 2752520 | tf_op jit(solution)/shard_map/ppermute | solution.py:31
  153.4 24.5 %collective-permute-start.9 = (bf16[64,7168]{1,0:T(8,128)(2,1)S(1)}, bf16[64,7168]{1,0:T(8,128)(2,1)S(1)}, u32[]{:S(2)}, u32[]{:S(2)}) collective-permute-start(bf16[64,7168]{1,0:T(8,128)(2,1)S(1)} %get-tuple-element.62), channel_id=1, source_target_pairs={{0,2},{1,3},{2,0},{3,1},{4,6},{5,7},{6,4},{7,5},{8,10},{9,11},{10,... | collective-permute-start | bytes 2752520 | tf_op jit(solution)/shard_map/ppermute | solution.py:31
  156.6 26.3 %collective-permute-start.10 = (bf16[32,7168]{1,0:T(8,128)(2,1)S(1)}, bf16[32,7168]{1,0:T(8,128)(2,1)S(1)}, u32[]{:S(2)}, u32[]{:S(2)}) collective-permute-start(bf16[32,7168]{1,0:T(8,128)(2,1)S(1)} %get-tuple-element.65), channel_id=1, source_target_pairs={{0,2},{1,3},{2,0},{3,1},{4,6},{5,7},{6,4},{7,5},{8,10},{9,11},{10,... | collective-permute-start | bytes 1376264 | tf_op jit(solution)/shard_map/ppermute | solution.py:31
  159.3 30.4 %collective-permute-start.8 = (bf16[32,7168]{1,0:T(8,128)(2,1)}, bf16[32,7168]{1,0:T(8,128)(2,1)}, u32[]{:S(2)}, u32[]{:S(2)}) collective-permute-start(bf16[32,7168]{1,0:T(8,128)(2,1)} %get-tuple-element.57), channel_id=1, source_target_pairs={{0,12},{1,13},{2,14},{3,15},{4,0},{5,1},{6,2},{7,3},{8,4},{9,5},{1... | collective-permute-start | bytes 1376264 | tf_op jit(solution)/shard_map/ppermute | solution.py:31
  162.5 27.2 %collective-permute-start.11 = (bf16[32,7168]{1,0:T(8,128)(2,1)}, bf16[32,7168]{1,0:T(8,128)(2,1)}, u32[]{:S(2)}, u32[]{:S(2)}) collective-permute-start(bf16[32,7168]{1,0:T(8,128)(2,1)} %get-tuple-element.59), channel_id=1, source_target_pairs={{0,4},{1,5},{2,6},{3,7},{4,8},{5,9},{6,10},{7,11},{8,12},{9,13},{1... | collective-permute-start | bytes 1376264 | tf_op jit(solution)/shard_map/ppermute | solution.py:31
  179.0 13.9 %collective-permute-start.14 = (bf16[32,7168]{1,0:T(8,128)(2,1)}, bf16[32,7168]{1,0:T(8,128)(2,1)}, u32[]{:S(2)}, u32[]{:S(2)}) collective-permute-start(bf16[32,7168]{1,0:T(8,128)(2,1)} %get-tuple-element.70), channel_id=1, source_target_pairs={{0,12},{1,13},{2,14},{3,15},{4,0},{5,1},{6,2},{7,3},{8,4},{9,5},{1... | collective-permute-start | bytes 1376264 | tf_op jit(solution)/shard_map/ppermute | solution.py:31
  183.7 27.2 %collective-permute-start.16 = (bf16[64,7168]{1,0:T(8,128)(2,1)}, bf16[64,7168]{1,0:T(8,128)(2,1)}, u32[]{:S(2)}, u32[]{:S(2)}) collective-permute-start(bf16[64,7168]{1,0:T(8,128)(2,1)} %get-tuple-element.75), channel_id=1, source_target_pairs={{0,2},{1,3},{2,0},{3,1},{4,6},{5,7},{6,4},{7,5},{8,10},{9,11},{10,... | collective-permute-start | bytes 2752520 | tf_op jit(solution)/shard_map/ppermute | solution.py:31
  195.9 31.0 %collective-permute-start.18 = (bf16[64,7296]{1,0:T(8,128)(2,1)S(1)}, bf16[64,7296]{1,0:T(8,128)(2,1)S(1)}, u32[]{:S(2)}, u32[]{:S(2)}) collective-permute-start(bf16[64,7296]{1,0:T(8,128)(2,1)S(1)} %shard_map.140), channel_id=1, source_target_pairs={{0,112},{1,113},{2,114},{3,115},{4,116},{5,117},{6,118},{7,119},{8... | collective-permute-start | bytes 2801672 | tf_op jit(solution)/shard_map/ppermute | solution.py:31
  200.0 33.3 %collective-permute-start.12 = (bf16[64,7296]{1,0:T(8,128)(2,1)S(1)}, bf16[64,7296]{1,0:T(8,128)(2,1)S(1)}, u32[]{:S(2)}, u32[]{:S(2)}) collective-permute-start(bf16[64,7296]{1,0:T(8,128)(2,1)S(1)} %shard_map.139), channel_id=1, source_target_pairs={{0,16},{1,17},{2,18},{3,19},{4,20},{5,21},{6,22},{7,23},{8,24},{9,... | collective-permute-start | bytes 2801672 | tf_op jit(solution)/shard_map/ppermute | solution.py:31
  203.3 29.2 %collective-permute-start.19 = (bf16[32,7168]{1,0:T(8,128)(2,1)S(1)}, bf16[32,7168]{1,0:T(8,128)(2,1)S(1)}, u32[]{:S(2)}, u32[]{:S(2)}) collective-permute-start(bf16[32,7168]{1,0:T(8,128)(2,1)S(1)} %copy-done.20), channel_id=1, source_target_pairs={{0,2},{1,3},{2,0},{3,1},{4,6},{5,7},{6,4},{7,5},{8,10},{9,11},{10,... | collective-permute-start | bytes 1376264 | tf_op jit(solution)/shard_map/ppermute | solution.py:31
  212.3 21.1 %collective-permute-start.17 = (bf16[32,7168]{1,0:T(8,128)(2,1)S(1)}, bf16[32,7168]{1,0:T(8,128)(2,1)S(1)}, u32[]{:S(2)}, u32[]{:S(2)}) collective-permute-start(bf16[32,7168]{1,0:T(8,128)(2,1)S(1)} %get-tuple-element.76), channel_id=1, source_target_pairs={{0,8},{1,9},{2,10},{3,11},{4,12},{5,13},{6,14},{7,15},{8,0},{9,1},... | collective-permute-start | bytes 1376264 | tf_op jit(solution)/shard_map/ppermute | solution.py:31
  233.7 22.6 %collective-permute-start.20 = (bf16[64,7296]{1,0:T(8,128)(2,1)S(1)}, bf16[64,7296]{1,0:T(8,128)(2,1)S(1)}, u32[]{:S(2)}, u32[]{:S(2)}) collective-permute-start(bf16[64,7296]{1,0:T(8,128)(2,1)S(1)} %shard_map.144), channel_id=1, source_target_pairs={{0,16},{1,17},{2,18},{3,19},{4,20},{5,21},{6,22},{7,23},{8,24},{9,... | collective-permute-start | bytes 2801672 | tf_op jit(solution)/shard_map/ppermute | solution.py:31
  233.8 14.2 %collective-permute-start.21 = (bf16[32,7296]{1,0:T(8,128)(2,1)S(1)}, bf16[32,7296]{1,0:T(8,128)(2,1)S(1)}, u32[]{:S(2)}, u32[]{:S(2)}) collective-permute-start(bf16[32,7296]{1,0:T(8,128)(2,1)S(1)} %shard_map.141), channel_id=1, source_target_pairs={{0,112},{1,113},{2,114},{3,115},{4,116},{5,117},{6,118},{7,119},{8... | collective-permute-start | bytes 1400840 | tf_op jit(solution)/shard_map/ppermute | solution.py:31
  240.9 12.1 %collective-permute-start.22 = (bf16[32,7296]{1,0:T(8,128)(2,1)S(1)}, bf16[32,7296]{1,0:T(8,128)(2,1)S(1)}, u32[]{:S(2)}, u32[]{:S(2)}) collective-permute-start(bf16[32,7296]{1,0:T(8,128)(2,1)S(1)} %shard_map.143), channel_id=1, source_target_pairs={{0,112},{1,113},{2,114},{3,115},{4,116},{5,117},{6,118},{7,119},{8... | collective-permute-start | bytes 1400840 | tf_op jit(solution)/shard_map/ppermute | solution.py:31
  (27 other events, 202.7 us)

commit v4 on v3

--- a/solution.py
+++ b/solution.py
@@ -108,21 +108,26 @@
 
 def unpick_kernel(*refs):
     *parts, out = refs
-    tokens, features = out.shape
-
-    def rows(here):
-        return jnp.concatenate([p[:, here] for p in parts], axis=0)
-
-    token = rows(slice(features, features + LANES)).astype(jnp.float32)
-    index = lax.broadcasted_iota(jnp.int32, (tokens, LANES), 1).astype(jnp.float32)
+    names, parts = parts[: len(parts) // 2], parts[len(parts) // 2 :]
+    token = jnp.concatenate([p[...] for p in names], axis=0).astype(jnp.float32)
+    index = lax.broadcasted_iota(jnp.int32, token.shape, 1).astype(jnp.float32)
     chosen = (token == index).astype(jnp.bfloat16).T
-    for j in range(0, features, WIDE):
-        here = slice(j, j + WIDE)
-        out[:, here] = dot(chosen, rows(here)).astype(jnp.bfloat16)
+    rows = jnp.concatenate([p[...] for p in parts], axis=0)
+    out[...] = dot(chosen, rows).astype(jnp.bfloat16)
 
 
 def unpick(parts, tokens, features):
-    return whole(unpick_kernel, table(tokens, features), *parts)
+    across = features // 4
+    return pl.pallas_call(
+        unpick_kernel,
+        grid=(4,),
+        out_shape=table(tokens, features),
+        in_specs=[pl.BlockSpec((p.shape[0], LANES), lambda i: (0, features // LANES)) for p in parts]
+        + [pl.BlockSpec((p.shape[0], across), lambda i: (0, i)) for p in parts],
+        out_specs=pl.BlockSpec((tokens, across), lambda i: (0, i)),
+        compiler_params=VMEM,
+        cost_estimate=LIGHT,
+    )(*parts, *parts)
 
 
 def sum_kernel(near, far, *outs):

time: 259 us -> 260 us (level)
    pallas_call x0 -> x2, Pallas kernels: none -> 6.02 us  [unpick(): pl.pallas_call(unpick_kernel, grid=(4,), out_shape=table(tokens, features...]
    pallas_call x14 -> x12, Pallas kernels: 22.3 us -> 18.5 us  [whole(): pl.pallas_call(kernel, out_shape=outs, in_specs=[pl.BlockSpec(memory_spac...]
where the time goes in v4:
time: 260 us; the launch traced here: 259 us
  waiting for transfers between devices  115 us (44%)
  starting transfers between devices  63.6 us (24%)
  Pallas kernels  55.2 us (21%)
  local copies, waits for them, and re-layouts  20.7 us (8%)
  other arithmetic  3.4 us (1%)
    ppermute x23, waiting for transfers between devices, move(): return lax.ppermute(block, ('pp', 'ep'), route)  95.6 us
    ppermute x23, starting transfers between devices, move(): return lax.ppermute(block, ('pp', 'ep'), route)  49.5 us
    pallas_call x2, Pallas kernels, through_expert(): pl.pallas_call(functools.partial(kernel, steps), grid=(2 * steps,), out_s...  30.7 us
    unnamed x50, local copies, waits for them, and re-layouts  20.1 us
    all_to_all x3, waiting for transfers between devices, along_y(): lax.all_to_all(rows.reshape(shape), 'ep', 0, 0, axis_index_groups=groups,...  19.8 us
    pallas_call x12, Pallas kernels, whole(): pl.pallas_call(kernel, out_shape=outs, in_specs=[pl.BlockSpec(memory_spac...  18.5 us
    all_to_all x3, starting transfers between devices, along_y(): lax.all_to_all(rows.reshape(shape), 'ep', 0, 0, axis_index_groups=groups,...  14 us
    pallas_call x2, Pallas kernels, unpick(): pl.pallas_call(unpick_kernel, grid=(4,), out_shape=table(tokens, features...  6.02 us
  transfers between devices with their start and end apart: 26, of which 12 were waited for; matrix products, arithmetic and copies ran while one was open for 2% of the time, Pallas kernels for 20%

profile of v4, /device:TPU:0, one launch (start us, length us, event | category | flops | bytes accessed | tf_op | source)
XLA Modules:
  0.0 259.2 jit_solution(564936834802624939)
XLA Ops:
  0.6 3.2 %collective-permute-start.4 = (bf16[128,7168]{1,0:T(8,128)(2,1)}, bf16[128,7168]{1,0:T(8,128)(2,1)}, u32[]{:S(2)}, u32[]{:S(2)}) collective-permute-start(bf16[128,7168]{1,0:T(8,128)(2,1)} %bitcast.31), channel_id=1, source_target_pairs={{0,2},{1,3},{2,0},{3,1},{4,6},{5,7},{6,4},{7,5},{8,10},{9,11},{10,... | collective-permute-start | bytes 5505032 | tf_op jit(solution)/shard_map/ppermute | solution.py:31
  11.8 4.6 %all-to-all-start = ((bf16[4,32,7168]{2,1,0:T(8,128)(2,1)}), bf16[4,32,7168]{2,1,0:T(8,128)(2,1)}, u32[]{:S(2)}, u32[]{:S(2)}) async-start(bf16[4,32,7168]{2,1,0:T(8,128)(2,1)} %bitcast.7), calls=%async_computation | async-start | bytes 3670016 | tf_op jit(solution)/shard_map/all_to_all | solution.py:320
  22.4 21.7 %collective-permute-done.5.far_order = s32[1,128]{1,0:T(1,128)S(1)} collective-permute-done((s32[1,128]{1,0:T(1,128)S(1)}, s32[1,128]{1,0:T(1,128)S(1)}, u32[]{:S(2)}, u32[]{:S(2)}) %collective-permute-start.5) | collective-permute-done | bytes 544 | tf_op jit(solution)/shard_map/ppermute | solution.py:31
  44.2 4.7 %all-to-all-start.1 = ((bf16[4,32,7168]{2,1,0:T(8,128)(2,1)}), bf16[4,32,7168]{2,1,0:T(8,128)(2,1)}, u32[]{:S(2)}, u32[]{:S(2)}) async-start(bf16[4,32,7168]{2,1,0:T(8,128)(2,1)} %bitcast.33), calls=%async_computation.1 | async-start | bytes 3670016 | tf_op jit(solution)/shard_map/all_to_all | solution.py:320
  51.9 19.8 %all-to-all-done.1 = bf16[4,32,7168]{2,1,0:T(8,128)(2,1)} async-done(((bf16[4,32,7168]{2,1,0:T(8,128)(2,1)}), bf16[4,32,7168]{2,1,0:T(8,128)(2,1)}, u32[]{:S(2)}, u32[]{:S(2)}) %all-to-all-start.1) | async-done | bytes 1835040 | tf_op jit(solution)/shard_map/all_to_all | solution.py:320
  79.3 4.7 %all-to-all-start.2 = ((bf16[4,64,7168]{2,1,0:T(8,128)(2,1)}), bf16[4,64,7168]{2,1,0:T(8,128)(2,1)}, u32[]{:S(2)}, u32[]{:S(2)}) async-start(bf16[4,64,7168]{2,1,0:T(8,128)(2,1)} %bitcast.30), calls=%async_computation.2 | async-start | bytes 7340032 | tf_op jit(solution)/shard_map/all_to_all | solution.py:320
  84.1 3.2 %collective-permute-start.6 = (bf16[128,7168]{1,0:T(8,128)(2,1)}, bf16[128,7168]{1,0:T(8,128)(2,1)S(1)}, u32[]{:S(2)}, u32[]{:S(2)}) collective-permute-start(bf16[128,7168]{1,0:T(8,128)(2,1)} %bitcast.17.near), channel_id=1, source_target_pairs={{0,2},{1,3},{2,0},{3,1},{4,6},{5,7},{6,4},{7,5},{8,10},{9,11},{10,... | collective-permute-start | bytes 5505032 | tf_op jit(solution)/shard_map/ppermute | solution.py:31
  87.2 6.4 %collective-permute-done.far = bf16[128,7168]{1,0:T(8,128)(2,1)} collective-permute-done((bf16[128,7168]{1,0:T(8,128)(2,1)}, bf16[128,7168]{1,0:T(8,128)(2,1)}, u32[]{:S(2)}, u32[]{:S(2)}) %collective-permute-start) | collective-permute-done | bytes 1835040 | tf_op jit(solution)/shard_map/ppermute | solution.py:31
  95.7 12.9 %shard_map.132 = (bf16[64,7168]{1,0:T(8,128)(2,1)S(1)}, bf16[64,7168]{1,0:T(8,128)(2,1)S(1)}, bf16[64,7168]{1,0:T(8,128)(2,1)}, bf16[64,7168]{1,0:T(8,128)(2,1)}) custom-call(s32[1]{0:T(128)} %bitcast.6.place, bf16[128,7168]{1,0:T(8,128)(2,1)} %bitcast.8.near, bf16[128,7168]{1,0:T(8,128)(2,1)} %collective-permute-done.far, bf16[7168,256]{1,0:T(8,128)(2,1)S(1)} %bitcast.29, ...), custom_call_target="tpu_custom_call" | custom-call | flops 1000 | bytes 1000 | tf_op jit(solution)/shard_map/pallas_call | solution.py:280
  112.6 20.3 %collective-permute-done.6.far = bf16[128,7168]{1,0:T(8,128)(2,1)S(1)} collective-permute-done((bf16[128,7168]{1,0:T(8,128)(2,1)}, bf16[128,7168]{1,0:T(8,128)(2,1)S(1)}, u32[]{:S(2)}, u32[]{:S(2)}) %collective-permute-start.6) | collective-permute-done | bytes 1835040 | tf_op jit(solution)/shard_map/ppermute | solution.py:31
  135.6 17.8 %shard_map.135 = (bf16[64,7168]{1,0:T(8,128)(2,1)S(1)}, bf16[32,7168]{1,0:T(8,128)(2,1)S(1)}, bf16[32,7168]{1,0:T(8,128)(2,1)S(1)}, bf16[64,7168]{1,0:T(8,128)(2...) custom-call(s32[1]{0:T(128)} %bitcast.6.place, bf16[128,7168]{1,0:T(8,128)(2,1)} %bitcast.17.near, ...), custom_call_target="tpu_custom_call" | custom-call | flops 1000 | bytes 1000 | tf_op jit(solution)/shard_map/pallas_call | solution.py:280
  153.4 3.1 %collective-permute-start.9 = (bf16[64,7168]{1,0:T(8,128)(2,1)S(1)}, bf16[64,7168]{1,0:T(8,128)(2,1)S(1)}, u32[]{:S(2)}, u32[]{:S(2)}) collective-permute-start(bf16[64,7168]{1,0:T(8,128)(2,1)S(1)} %get-tuple-element.62), channel_id=1, source_target_pairs={{0,2},{1,3},{2,0},{3,1},{4,6},{5,7},{6,4},{7,5},{8,10},{9,11},{10,... | collective-permute-start | bytes 2752520 | tf_op jit(solution)/shard_map/ppermute | solution.py:31
  159.3 3.2 %collective-permute-start.8 = (bf16[32,7168]{1,0:T(8,128)(2,1)}, bf16[32,7168]{1,0:T(8,128)(2,1)}, u32[]{:S(2)}, u32[]{:S(2)}) collective-permute-start(bf16[32,7168]{1,0:T(8,128)(2,1)} %get-tuple-element.57), channel_id=1, source_target_pairs={{0,12},{1,13},{2,14},{3,15},{4,0},{5,1},{6,2},{7,3},{8,4},{9,5},{1... | collective-permute-start | bytes 1376264 | tf_op jit(solution)/shard_map/ppermute | solution.py:31
  162.5 15.4 %collective-permute-done.9.far = bf16[64,7168]{1,0:T(8,128)(2,1)S(1)} collective-permute-done((bf16[64,7168]{1,0:T(8,128)(2,1)S(1)}, bf16[64,7168]{1,0:T(8,128)(2,1)S(1)}, u32[]{:S(2)}, u32[]{:S(2)}) %collective-permute-start.9) | collective-permute-done | bytes 917536 | tf_op jit(solution)/shard_map/ppermute | solution.py:31
  183.7 3.2 %collective-permute-start.16 = (bf16[64,7168]{1,0:T(8,128)(2,1)}, bf16[64,7168]{1,0:T(8,128)(2,1)}, u32[]{:S(2)}, u32[]{:S(2)}) collective-permute-start(bf16[64,7168]{1,0:T(8,128)(2,1)} %get-tuple-element.75), channel_id=1, source_target_pairs={{0,2},{1,3},{2,0},{3,1},{4,6},{5,7},{6,4},{7,5},{8,10},{9,11},{10,... | collective-permute-start | bytes 2752520 | tf_op jit(solution)/shard_map/ppermute | solution.py:31
  195.9 4.1 %collective-permute-start.18 = (bf16[64,7296]{1,0:T(8,128)(2,1)S(1)}, bf16[64,7296]{1,0:T(8,128)(2,1)S(1)}, u32[]{:S(2)}, u32[]{:S(2)}) collective-permute-start(bf16[64,7296]{1,0:T(8,128)(2,1)S(1)} %shard_map.140), channel_id=1, source_target_pairs={{0,112},{1,113},{2,114},{3,115},{4,116},{5,117},{6,118},{7,119},{8... | collective-permute-start | bytes 2801672 | tf_op jit(solution)/shard_map/ppermute | solution.py:31
  200.0 3.3 %collective-permute-start.13 = (bf16[32,7168]{1,0:T(8,128)(2,1)S(1)}, bf16[32,7168]{1,0:T(8,128)(2,1)S(1)}, u32[]{:S(2)}, u32[]{:S(2)}) collective-permute-start(bf16[32,7168]{1,0:T(8,128)(2,1)S(1)} %shard_map.138), channel_id=1, source_target_pairs={{0,8},{1,9},{2,10},{3,11},{4,12},{5,13},{6,14},{7,15},{8,0},{9,1},... | collective-permute-start | bytes 1376264 | tf_op jit(solution)/shard_map/ppermute | solution.py:31
  205.3 4.7 %collective-permute-done.13.refs_0_ = bf16[32,7168]{1,0:T(8,128)(2,1)S(1)} collective-permute-done((bf16[32,7168]{1,0:T(8,128)(2,1)S(1)}, bf16[32,7168]{1,0:T(8,128)(2,1)S(1)}, u32[]{:S(2)}, u32[]{:S(2)}) %collective-permute-start.13) | collective-permute-done | bytes 458784 | tf_op jit(solution)/shard_map/ppermute | solution.py:31
  212.3 4.3 %collective-permute-start.17 = (bf16[32,7168]{1,0:T(8,128)(2,1)S(1)}, bf16[32,7168]{1,0:T(8,128)(2,1)S(1)}, u32[]{:S(2)}, u32[]{:S(2)}) collective-permute-start(bf16[32,7168]{1,0:T(8,128)(2,1)S(1)} %get-tuple-element.76), channel_id=1, source_target_pairs={{0,8},{1,9},{2,10},{3,11},{4,12},{5,13},{6,14},{7,15},{8,0},{9,1},... | collective-permute-start | bytes 1376264 | tf_op jit(solution)/shard_map/ppermute | solution.py:31
  216.6 10.3 %collective-permute-done.18.refs_0_.refs_3_ = bf16[64,7296]{1,0:T(8,128)(2,1)S(1)} collective-permute-done((bf16[64,7296]{1,0:T(8,128)(2,1)S(1)}, bf16[64,7296]{1,0:T(8,128)(2,1)S(1)}, u32[]{:S(2)}, u32[]{:S(2)}) %collective-permute-start.18) | collective-permute-done | bytes 933920 | tf_op jit(solution)/shard_map/ppermute | solution.py:31
  226.9 5.7 %collective-permute-done.19.refs_1_ = bf16[32,7168]{1,0:T(8,128)(2,1)S(1)} collective-permute-done((bf16[32,7168]{1,0:T(8,128)(2,1)S(1)}, bf16[32,7168]{1,0:T(8,128)(2,1)S(1)}, u32[]{:S(2)}, u32[]{:S(2)}) %collective-permute-start.19) | collective-permute-done | bytes 458784 | tf_op jit(solution)/shard_map/ppermute | solution.py:31
  233.8 7.1 %collective-permute-start.21 = (bf16[32,7296]{1,0:T(8,128)(2,1)S(1)}, bf16[32,7296]{1,0:T(8,128)(2,1)S(1)}, u32[]{:S(2)}, u32[]{:S(2)}) collective-permute-start(bf16[32,7296]{1,0:T(8,128)(2,1)S(1)} %shard_map.141), channel_id=1, source_target_pairs={{0,112},{1,113},{2,114},{3,115},{4,116},{5,117},{6,118},{7,119},{8... | collective-permute-start | bytes 1400840 | tf_op jit(solution)/shard_map/ppermute | solution.py:31
  242.8 5.2 %collective-permute-done.21.refs_1_.refs_4_ = bf16[32,7296]{1,0:T(8,128)(2,1)S(1)} collective-permute-done((bf16[32,7296]{1,0:T(8,128)(2,1)S(1)}, bf16[32,7296]{1,0:T(8,128)(2,1)S(1)}, u32[]{:S(2)}, u32[]{:S(2)}) %collective-permute-start.21) | collective-permute-done | bytes 466976 | tf_op jit(solution)/shard_map/ppermute | solution.py:31
  248.0 5.0 %collective-permute-done.22.refs_2_.refs_5_ = bf16[32,7296]{1,0:T(8,128)(2,1)S(1)} collective-permute-done((bf16[32,7296]{1,0:T(8,128)(2,1)S(1)}, bf16[32,7296]{1,0:T(8,128)(2,1)S(1)}, u32[]{:S(2)}, u32[]{:S(2)}) %collective-permute-start.22) | collective-permute-done | bytes 466976 | tf_op jit(solution)/shard_map/ppermute | solution.py:31
  (113 shorter events, 64.3 us)
Async XLA Ops:
  0.6 43.5 %collective-permute-start.4 = (bf16[128,7168]{1,0:T(8,128)(2,1)}, bf16[128,7168]{1,0:T(8,128)(2,1)}, u32[]{:S(2)}, u32[]{:S(2)}) collective-permute-start(bf16[128,7168]{1,0:T(8,128)(2,1)} %bitcast.31), channel_id=1, source_target_pairs={{0,2},{1,3},{2,0},{3,1},{4,6},{5,7},{6,4},{7,5},{8,10},{9,11},{10,... | collective-permute-start | bytes 5505032 | tf_op jit(solution)/shard_map/ppermute | solution.py:31
  11.8 32.3 %all-to-all-start = ((bf16[4,32,7168]{2,1,0:T(8,128)(2,1)}), bf16[4,32,7168]{2,1,0:T(8,128)(2,1)}, u32[]{:S(2)}, u32[]{:S(2)}) async-start(bf16[4,32,7168]{2,1,0:T(8,128)(2,1)} %bitcast.7), calls=%async_computation | async-start | bytes 3670016 | tf_op jit(solution)/shard_map/all_to_all | solution.py:320
  16.4 77.2 %collective-permute-start.1 = (bf16[7168,256]{1,0:T(8,128)(2,1)}, bf16[7168,256]{1,0:T(8,128)(2,1)}, u32[]{:S(2)}, u32[]{:S(2)}) collective-permute-start(bf16[7168,256]{1,0:T(8,128)(2,1)} %bitcast.27), channel_id=1, source_target_pairs={{0,1},{1,0},{2,3},{3,2},{4,5},{5,4},{6,7},{7,6},{8,9},{9,8},{10,11... | collective-permute-start | bytes 11010056 | tf_op jit(solution)/shard_map/ppermute | solution.py:31
  16.5 77.2 %collective-permute-start.2 = (bf16[7168,256]{1,0:T(8,128)(2,1)}, bf16[7168,256]{1,0:T(8,128)(2,1)}, u32[]{:S(2)}, u32[]{:S(2)}) collective-permute-start(bf16[7168,256]{1,0:T(8,128)(2,1)} %bitcast.39), channel_id=1, source_target_pairs={{0,1},{1,0},{2,3},{3,2},{4,5},{5,4},{6,7},{7,6},{8,9},{9,8},{10,11... | collective-permute-start | bytes 11010056 | tf_op jit(solution)/shard_map/ppermute | solution.py:31
  17.0 76.7 %collective-permute-start.3 = (bf16[256,7168]{1,0:T(8,128)(2,1)}, bf16[256,7168]{1,0:T(8,128)(2,1)}, u32[]{:S(2)}, u32[]{:S(2)}) collective-permute-start(bf16[256,7168]{1,0:T(8,128)(2,1)} %bitcast.42), channel_id=1, source_target_pairs={{0,1},{1,0},{2,3},{3,2},{4,5},{5,4},{6,7},{7,6},{8,9},{9,8},{10,11... | collective-permute-start | bytes 11010056 | tf_op jit(solution)/shard_map/ppermute | solution.py:31
  17.1 27.1 %collective-permute-start.5 = (s32[1,128]{1,0:T(1,128)S(1)}, s32[1,128]{1,0:T(1,128)S(1)}, u32[]{:S(2)}, u32[]{:S(2)}) collective-permute-start(s32[1,128]{1,0:T(1,128)S(1)} %multiply_add_fusion.expert_order.near_order), channel_id=1, source_target_pairs={{0,2},{1,3},{2,0},{3,1},{4,6},{5,7},{6,4},{7,5},{8,10},{9,11},{10,... | collective-permute-start | bytes 1544 | tf_op jit(solution)/shard_map/ppermute | solution.py:31
  44.2 27.5 %all-to-all-start.1 = ((bf16[4,32,7168]{2,1,0:T(8,128)(2,1)}), bf16[4,32,7168]{2,1,0:T(8,128)(2,1)}, u32[]{:S(2)}, u32[]{:S(2)}) async-start(bf16[4,32,7168]{2,1,0:T(8,128)(2,1)} %bitcast.33), calls=%async_computation.1 | async-start | bytes 3670016 | tf_op jit(solution)/shard_map/all_to_all | solution.py:320
  48.8 44.8 %collective-permute-start = (bf16[128,7168]{1,0:T(8,128)(2,1)}, bf16[128,7168]{1,0:T(8,128)(2,1)}, u32[]{:S(2)}, u32[]{:S(2)}) collective-permute-start(bf16[128,7168]{1,0:T(8,128)(2,1)} %bitcast.8.near), channel_id=1, source_target_pairs={{0,2},{1,3},{2,0},{3,1},{4,6},{5,7},{6,4},{7,5},{8,10},{9,11},{10,... | collective-permute-start | bytes 5505032 | tf_op jit(solution)/shard_map/ppermute | solution.py:31
  79.3 54.8 %all-to-all-start.2 = ((bf16[4,64,7168]{2,1,0:T(8,128)(2,1)}), bf16[4,64,7168]{2,1,0:T(8,128)(2,1)}, u32[]{:S(2)}, u32[]{:S(2)}) async-start(bf16[4,64,7168]{2,1,0:T(8,128)(2,1)} %bitcast.30), calls=%async_computation.2 | async-start | bytes 7340032 | tf_op jit(solution)/shard_map/all_to_all | solution.py:320
  84.1 48.8 %collective-permute-start.6 = (bf16[128,7168]{1,0:T(8,128)(2,1)}, bf16[128,7168]{1,0:T(8,128)(2,1)S(1)}, u32[]{:S(2)}, u32[]{:S(2)}) collective-permute-start(bf16[128,7168]{1,0:T(8,128)(2,1)} %bitcast.17.near), channel_id=1, source_target_pairs={{0,2},{1,3},{2,0},{3,1},{4,6},{5,7},{6,4},{7,5},{8,10},{9,11},{10,... | collective-permute-start | bytes 5505032 | tf_op jit(solution)/shard_map/ppermute | solution.py:31
  109.5 43.9 %collective-permute-start.7 = (bf16[64,7168]{1,0:T(8,128)(2,1)}, bf16[64,7168]{1,0:T(8,128)(2,1)}, u32[]{:S(2)}, u32[]{:S(2)}) collective-permute-start(bf16[64,7168]{1,0:T(8,128)(2,1)} %get-tuple-element.56), channel_id=1, source_target_pairs={{0,2},{1,3},{2,0},{3,1},{4,6},{5,7},{6,4},{7,5},{8,10},{9,11},{10,... | collective-permute-start | bytes 2752520 | tf_op jit(solution)/shard_map/ppermute | solution.py:31
  153.4 24.5 %collective-permute-start.9 = (bf16[64,7168]{1,0:T(8,128)(2,1)S(1)}, bf16[64,7168]{1,0:T(8,128)(2,1)S(1)}, u32[]{:S(2)}, u32[]{:S(2)}) collective-permute-start(bf16[64,7168]{1,0:T(8,128)(2,1)S(1)} %get-tuple-element.62), channel_id=1, source_target_pairs={{0,2},{1,3},{2,0},{3,1},{4,6},{5,7},{6,4},{7,5},{8,10},{9,11},{10,... | collective-permute-start | bytes 2752520 | tf_op jit(solution)/shard_map/ppermute | solution.py:31
  156.6 26.3 %collective-permute-start.10 = (bf16[32,7168]{1,0:T(8,128)(2,1)S(1)}, bf16[32,7168]{1,0:T(8,128)(2,1)S(1)}, u32[]{:S(2)}, u32[]{:S(2)}) collective-permute-start(bf16[32,7168]{1,0:T(8,128)(2,1)S(1)} %get-tuple-element.65), channel_id=1, source_target_pairs={{0,2},{1,3},{2,0},{3,1},{4,6},{5,7},{6,4},{7,5},{8,10},{9,11},{10,... | collective-permute-start | bytes 1376264 | tf_op jit(solution)/shard_map/ppermute | solution.py:31
  159.3 30.4 %collective-permute-start.8 = (bf16[32,7168]{1,0:T(8,128)(2,1)}, bf16[32,7168]{1,0:T(8,128)(2,1)}, u32[]{:S(2)}, u32[]{:S(2)}) collective-permute-start(bf16[32,7168]{1,0:T(8,128)(2,1)} %get-tuple-element.57), channel_id=1, source_target_pairs={{0,12},{1,13},{2,14},{3,15},{4,0},{5,1},{6,2},{7,3},{8,4},{9,5},{1... | collective-permute-start | bytes 1376264 | tf_op jit(solution)/shard_map/ppermute | solution.py:31
  162.5 27.2 %collective-permute-start.11 = (bf16[32,7168]{1,0:T(8,128)(2,1)}, bf16[32,7168]{1,0:T(8,128)(2,1)}, u32[]{:S(2)}, u32[]{:S(2)}) collective-permute-start(bf16[32,7168]{1,0:T(8,128)(2,1)} %get-tuple-element.59), channel_id=1, source_target_pairs={{0,4},{1,5},{2,6},{3,7},{4,8},{5,9},{6,10},{7,11},{8,12},{9,13},{1... | collective-permute-start | bytes 1376264 | tf_op jit(solution)/shard_map/ppermute | solution.py:31
  179.0 13.9 %collective-permute-start.14 = (bf16[32,7168]{1,0:T(8,128)(2,1)}, bf16[32,7168]{1,0:T(8,128)(2,1)}, u32[]{:S(2)}, u32[]{:S(2)}) collective-permute-start(bf16[32,7168]{1,0:T(8,128)(2,1)} %get-tuple-element.70), channel_id=1, source_target_pairs={{0,12},{1,13},{2,14},{3,15},{4,0},{5,1},{6,2},{7,3},{8,4},{9,5},{1... | collective-permute-start | bytes 1376264 | tf_op jit(solution)/shard_map/ppermute | solution.py:31
  183.7 27.2 %collective-permute-start.16 = (bf16[64,7168]{1,0:T(8,128)(2,1)}, bf16[64,7168]{1,0:T(8,128)(2,1)}, u32[]{:S(2)}, u32[]{:S(2)}) collective-permute-start(bf16[64,7168]{1,0:T(8,128)(2,1)} %get-tuple-element.75), channel_id=1, source_target_pairs={{0,2},{1,3},{2,0},{3,1},{4,6},{5,7},{6,4},{7,5},{8,10},{9,11},{10,... | collective-permute-start | bytes 2752520 | tf_op jit(solution)/shard_map/ppermute | solution.py:31
  195.9 31.0 %collective-permute-start.18 = (bf16[64,7296]{1,0:T(8,128)(2,1)S(1)}, bf16[64,7296]{1,0:T(8,128)(2,1)S(1)}, u32[]{:S(2)}, u32[]{:S(2)}) collective-permute-start(bf16[64,7296]{1,0:T(8,128)(2,1)S(1)} %shard_map.140), channel_id=1, source_target_pairs={{0,112},{1,113},{2,114},{3,115},{4,116},{5,117},{6,118},{7,119},{8... | collective-permute-start | bytes 2801672 | tf_op jit(solution)/shard_map/ppermute | solution.py:31
  200.0 33.3 %collective-permute-start.12 = (bf16[64,7296]{1,0:T(8,128)(2,1)S(1)}, bf16[64,7296]{1,0:T(8,128)(2,1)S(1)}, u32[]{:S(2)}, u32[]{:S(2)}) collective-permute-start(bf16[64,7296]{1,0:T(8,128)(2,1)S(1)} %shard_map.139), channel_id=1, source_target_pairs={{0,16},{1,17},{2,18},{3,19},{4,20},{5,21},{6,22},{7,23},{8,24},{9,... | collective-permute-start | bytes 2801672 | tf_op jit(solution)/shard_map/ppermute | solution.py:31
  203.3 29.2 %collective-permute-start.19 = (bf16[32,7168]{1,0:T(8,128)(2,1)S(1)}, bf16[32,7168]{1,0:T(8,128)(2,1)S(1)}, u32[]{:S(2)}, u32[]{:S(2)}) collective-permute-start(bf16[32,7168]{1,0:T(8,128)(2,1)S(1)} %copy-done.20), channel_id=1, source_target_pairs={{0,2},{1,3},{2,0},{3,1},{4,6},{5,7},{6,4},{7,5},{8,10},{9,11},{10,... | collective-permute-start | bytes 1376264 | tf_op jit(solution)/shard_map/ppermute | solution.py:31
  212.3 21.1 %collective-permute-start.17 = (bf16[32,7168]{1,0:T(8,128)(2,1)S(1)}, bf16[32,7168]{1,0:T(8,128)(2,1)S(1)}, u32[]{:S(2)}, u32[]{:S(2)}) collective-permute-start(bf16[32,7168]{1,0:T(8,128)(2,1)S(1)} %get-tuple-element.76), channel_id=1, source_target_pairs={{0,8},{1,9},{2,10},{3,11},{4,12},{5,13},{6,14},{7,15},{8,0},{9,1},... | collective-permute-start | bytes 1376264 | tf_op jit(solution)/shard_map/ppermute | solution.py:31
  233.7 22.6 %collective-permute-start.20 = (bf16[64,7296]{1,0:T(8,128)(2,1)S(1)}, bf16[64,7296]{1,0:T(8,128)(2,1)S(1)}, u32[]{:S(2)}, u32[]{:S(2)}) collective-permute-start(bf16[64,7296]{1,0:T(8,128)(2,1)S(1)} %shard_map.144), channel_id=1, source_target_pairs={{0,16},{1,17},{2,18},{3,19},{4,20},{5,21},{6,22},{7,23},{8,24},{9,... | collective-permute-start | bytes 2801672 | tf_op jit(solution)/shard_map/ppermute | solution.py:31
  233.8 14.2 %collective-permute-start.21 = (bf16[32,7296]{1,0:T(8,128)(2,1)S(1)}, bf16[32,7296]{1,0:T(8,128)(2,1)S(1)}, u32[]{:S(2)}, u32[]{:S(2)}) collective-permute-start(bf16[32,7296]{1,0:T(8,128)(2,1)S(1)} %shard_map.141), channel_id=1, source_target_pairs={{0,112},{1,113},{2,114},{3,115},{4,116},{5,117},{6,118},{7,119},{8... | collective-permute-start | bytes 1400840 | tf_op jit(solution)/shard_map/ppermute | solution.py:31
  240.9 12.1 %collective-permute-start.22 = (bf16[32,7296]{1,0:T(8,128)(2,1)S(1)}, bf16[32,7296]{1,0:T(8,128)(2,1)S(1)}, u32[]{:S(2)}, u32[]{:S(2)}) collective-permute-start(bf16[32,7296]{1,0:T(8,128)(2,1)S(1)} %shard_map.143), channel_id=1, source_target_pairs={{0,112},{1,113},{2,114},{3,115},{4,116},{5,117},{6,118},{7,119},{8... | collective-permute-start | bytes 1400840 | tf_op jit(solution)/shard_map/ppermute | solution.py:31
  (27 other events, 202.7 us)
